TPU v7x, 32 devices: a whole 2x2x4 slice. The times are simulated.
32 devices in a mesh: dp: 16 (over z, y, core), sub: 2 (over x).
Axes of the slice: x: 2, y: 2, z: 4, core: 2. Of those that a mesh axis runs over, the one named last changes fastest.
Arguments:
- features: bfloat16 [16, 2, 300, 25, 256], P('dp', None, None, None, 'sub'), may hold values from -12 to 12
- presence: int32 [16, 2], P('dp'), may hold values from 0 to 1
- parents: int32 [25], replicated, may hold values from 0 to 23, as said below
- w_spatial: bfloat16 [256, 768], P(None, 'sub'), may hold values from -0.375 to 0.375
- importance: float32 [3, 25, 25], replicated, may hold values from 0.5 to 1.5
- gain_one: float32 [256], P('sub'), may hold values from 0.25 to 1.75
- shift_one: float32 [256], P('sub'), may hold values from -0.5 to 0.5
- w_temporal: bfloat16 [9, 256, 256], P(None, None, 'sub'), may hold values from -0.125 to 0.125
- gain_two: float32 [256], P('sub'), may hold values from 0.25 to 1.75
- shift_two: float32 [256], P('sub'), may hold values from -0.5 to 0.5
- cotangent: bfloat16 [16, 2, 300, 25, 256], P('dp', None, None, None, 'sub'), may hold values from -6 to 6
Outputs:
- activations: float32 [16, 2, 300, 25, 256], P('dp', None, None, None, 'sub')
- input_grad: float32 [16, 2, 300, 25, 256], P('dp', None, None, None, 'sub')
- spatial_grad: float32 [256, 768], P(None, 'sub')
- importance_grad: float32 [3, 25, 25], replicated
- gain_one_grad: float32 [256], P('sub')
- shift_one_grad: float32 [256], P('sub')
- temporal_grad: float32 [9, 256, 256], P(None, None, 'sub')
- gain_two_grad: float32 [256], P('sub')
- shift_two_grad: float32 [256], P('sub')
Inputs may be any that keep to these rules, and one draw needn't show every extreme that they name: `parents`: entry 0 is 0, entry v is below v for v >= 1, and entry 24 is 23, so the entries form a tree rooted at joint 0.
All inputs are finite; a program needn't handle non-finite values.
Results may differ from a plain program's by a relative error of at most 0.0069.
Values may be sent and summed in bfloat16 or wider, within the bound.
A program may use at most 320 MiB of HBM per device.

v0:
```python
import jax
import jax.numpy as jnp
from jax import lax
from jax.sharding import PartitionSpec as P

norm_eps = 1e-05
exact_mode = lax.Precision.HIGHEST
row_contract = (((0,), (0,)), ((), ()))
column_contract = (((1,), (1,)), ((), ()))


def adjacency(parents):
    joints = parents.shape[0]
    position = jnp.arange(joints, dtype=jnp.int32)
    toward = ((position[None, :] == parents[:, None]) & (position[:, None] != 0)).astype(
        jnp.float32
    )
    stacked = jnp.stack([jnp.eye(joints, dtype=jnp.float32), toward, toward.T])
    degree = jnp.sum(stacked, axis=(0, 1))
    return stacked / degree[None, None, :]


def flatten_rows(values):
    return values.reshape(-1, values.shape[-1])


def statistics(values, present_weight, local_count):
    summed_up, counted = lax.psum(
        (jnp.sum(values * present_weight, axis=(0, 1, 2, 3)), local_count), "dp"
    )
    average = summed_up / counted
    centered = values - average
    variance = (
        lax.psum(jnp.sum(centered * centered * present_weight, axis=(0, 1, 2, 3)), "dp") / counted
    )
    inv_spread = lax.rsqrt(variance + norm_eps)
    return (centered * inv_spread, inv_spread, counted)


def norm_back(grad_out, normed, inv_spread, gain_vec, present_weight, counted):
    gain_grad, shift_grad = lax.psum(
        (jnp.sum(grad_out * normed, axis=(0, 1, 2, 3)), jnp.sum(grad_out, axis=(0, 1, 2, 3))), "dp"
    )
    grad_in = (
        gain_vec
        * inv_spread
        * (grad_out - present_weight * (shift_grad + normed * gain_grad) / counted)
    )
    return (grad_in, gain_grad, shift_grad)


def pad_frames(values, half_taps):
    return jnp.pad(values, ((0, 0), (0, 0), (half_taps, half_taps), (0, 0), (0, 0)))


def temporal(activity, weights):
    tap_count = weights.shape[0]
    frames = activity.shape[2]
    padded = pad_frames(activity, tap_count // 2)
    running = jnp.zeros(
        (activity.shape[0] * activity.shape[1] * frames * activity.shape[3], weights.shape[2]),
        jnp.float32,
    )
    for tap_index in range(tap_count):
        window = padded[:, :, tap_index : tap_index + frames]
        running = running + jnp.dot(
            flatten_rows(window), weights[tap_index], preferred_element_type=jnp.float32
        )
    return running


def temporal_weight_grad(activity, gradient, tap_count):
    frames = activity.shape[2]
    padded = pad_frames(activity, tap_count // 2)
    results = []
    for tap_index in range(tap_count):
        window = padded[:, :, tap_index : tap_index + frames]
        results.append(
            lax.dot_general(
                flatten_rows(window), gradient, row_contract, preferred_element_type=jnp.float32
            )
        )
    return jnp.stack(results)


def temporal_input_grad(gradient, weights):
    tap_count = weights.shape[0]
    frames = gradient.shape[2]
    padded = pad_frames(gradient, tap_count // 2)
    running = jnp.zeros(
        (gradient.shape[0] * gradient.shape[1] * frames * gradient.shape[3], weights.shape[1]),
        jnp.float32,
    )
    for tap_index in range(tap_count):
        anchor = tap_count - 1 - tap_index
        window = padded[:, :, anchor : anchor + frames]
        running = running + lax.dot_general(
            flatten_rows(window),
            weights[tap_index],
            column_contract,
            preferred_element_type=jnp.float32,
        )
    return running


def local(
    features,
    presence,
    parents,
    w_spatial,
    importance,
    gain_one,
    shift_one,
    w_temporal,
    gain_two,
    shift_two,
    cotangent,
):
    sub_count = lax.axis_size("sub")
    position = lax.axis_index("sub")
    channels = w_spatial.shape[0]
    columns = w_spatial.shape[1]
    group_width = columns // 3
    tap_count = w_temporal.shape[0]
    leading = features.shape[:4]
    groups = position * 3 + jnp.arange(3, dtype=jnp.int32)
    select = (groups[:, None] // sub_count == jnp.arange(3, dtype=jnp.int32)[None, :]).astype(
        jnp.float32
    )
    placing = (
        groups[:, None] % sub_count == jnp.arange(sub_count, dtype=jnp.int32)[None, :]
    ).astype(jnp.float32)
    adjacent = adjacency(parents)
    mixing = adjacent * importance
    local_mix = jnp.einsum("gk,kvw->gvw", select, mixing, precision=exact_mode)
    present_weight = presence.astype(jnp.float32)[:, :, None, None, None]
    local_count = jnp.sum(presence.astype(jnp.float32)) * (features.shape[2] * features.shape[3])
    whole_inputs = lax.all_gather(features, "sub", axis=4, tiled=True)
    spatial = jnp.dot(flatten_rows(whole_inputs), w_spatial, preferred_element_type=jnp.float32)
    grouped = spatial.reshape(leading + (3, group_width))
    mixed = jnp.einsum("gvw,aptwgc->aptvgc", local_mix, grouped, precision=exact_mode)
    term = jnp.einsum("gq,aptvgc->aptvqc", placing, mixed, precision=exact_mode)
    term = term.reshape(leading + (sub_count * group_width,))
    summed = lax.psum_scatter(term, "sub", scatter_dimension=4, tiled=True)
    normed_one, inv_one, counted = statistics(summed, present_weight, local_count)
    level_one = normed_one * gain_one + shift_one
    activity_full, gelu_one = jax.vjp(jax.nn.gelu, level_one)
    activity = activity_full.astype(jnp.bfloat16)
    whole_activity = lax.all_gather(activity, "sub", axis=4, tiled=True)
    conv = temporal(whole_activity, w_temporal)
    conv = conv.reshape(leading + (w_temporal.shape[2],))
    normed_two, inv_two, counted = statistics(conv, present_weight, local_count)
    level_two = normed_two * gain_two + shift_two + features.astype(jnp.float32)
    output, gelu_two = jax.vjp(jax.nn.gelu, level_two)
    grad_pre = gelu_two(cotangent.astype(jnp.float32))[0]
    grad_conv, gain_two_grad, shift_two_grad = norm_back(
        grad_pre, normed_two, inv_two, gain_two, present_weight, counted
    )
    grad_conv = grad_conv.astype(jnp.bfloat16)
    conv_rows = flatten_rows(grad_conv)
    temporal_grad = temporal_weight_grad(whole_activity, conv_rows, tap_count)
    grad_activity_full = temporal_input_grad(grad_conv, w_temporal).reshape(
        leading + (w_temporal.shape[1],)
    )
    grad_activity = lax.psum_scatter(grad_activity_full, "sub", scatter_dimension=4, tiled=True)
    grad_level = gelu_one(grad_activity)[0]
    grad_sum, gain_one_grad, shift_one_grad = norm_back(
        grad_level, normed_one, inv_one, gain_one, present_weight, counted
    )
    grad_whole = lax.all_gather(grad_sum.astype(jnp.bfloat16), "sub", axis=4, tiled=True)
    blocks = grad_whole.reshape(leading + (sub_count, group_width))
    chosen = jnp.einsum(
        "gq,aptvqc->aptvgc",
        placing.astype(jnp.bfloat16),
        blocks,
        preferred_element_type=jnp.float32,
    )
    grad_spatial = jnp.einsum("gvw,aptvgc->aptwgc", local_mix, chosen, precision=exact_mode)
    mix_grad = jnp.einsum("aptvgc,aptwgc->gvw", chosen, grouped, precision=exact_mode)
    importance_local = jnp.einsum("gk,gvw->kvw", select, mix_grad, precision=exact_mode) * adjacent
    grad_low = grad_spatial.astype(jnp.bfloat16).reshape(-1, columns)
    spatial_grad = lax.dot_general(
        flatten_rows(whole_inputs), grad_low, row_contract, preferred_element_type=jnp.float32
    )
    input_part = lax.dot_general(
        grad_low, w_spatial, column_contract, preferred_element_type=jnp.float32
    )
    input_part = input_part.reshape(leading + (channels,))
    input_grad = (
        lax.psum_scatter(
            input_part.astype(jnp.bfloat16), "sub", scatter_dimension=4, tiled=True
        ).astype(jnp.float32)
        + grad_pre
    )
    temporal_grad, spatial_grad = lax.psum((temporal_grad, spatial_grad), "dp")
    importance_grad = lax.psum(importance_local, ("dp", "sub"))
    return (
        output,
        input_grad,
        spatial_grad,
        importance_grad,
        gain_one_grad,
        shift_one_grad,
        temporal_grad,
        gain_two_grad,
        shift_two_grad,
    )


def solution(mesh):
    in_specs = (
        P("dp", None, None, None, "sub"),
        P("dp", None),
        P(),
        P(None, "sub"),
        P(),
        P("sub"),
        P("sub"),
        P(None, None, "sub"),
        P("sub"),
        P("sub"),
        P("dp", None, None, None, "sub"),
    )
    out_specs = (
        P("dp", None, None, None, "sub"),
        P("dp", None, None, None, "sub"),
        P(None, "sub"),
        P(),
        P("sub"),
        P("sub"),
        P(None, None, "sub"),
        P("sub"),
        P("sub"),
    )
    return jax.shard_map(local, mesh=mesh, in_specs=in_specs, out_specs=out_specs, check_vma=False)
```

profile of v0, /device:TPU:1, one launch (start us, length us, event | category | flops | bytes accessed | tf_op | source)
XLA Modules:
  0.0 1925.7 jit_solution(18082240626056380258)
XLA Ops:
  13.3 97.9 %all-gather.4.cloned.1.call-done = bf16[1,2,300,25,256]{4,2,3,1,0:T(8,128)(2,1)} async-done(((bf16[1,2,300,25,128]{4,2,3,1,0:T(8,128)(2,1)}), bf16[1,2,300,25,256]{4,2,3,1,0:T(8,128)(2,1)}) %all-gather.4.cloned.1.call-update) | async-done | bytes 7680016 | tf_op jit(solution)/shard_map/all_gather | solution.py:138
  111.2 13.8 fusion.32
  125.0 53.3 %fusion.12 = f32[2,300,25,3,128]{4,2,1,0,3:T(8,128)} fusion(f32[3,25,25,1,1]{1,2,4,3,0:T(8,128)S(1)} %copy.171, f32[2,300,25,3,128]{4,1,3,2,0:T(8,128)} %fusion.32), kind=kOutput, calls=%fused_computation.34 | convolution fusion | flops 1728000000 | bytes 46087500 | tf_op jit(solution)/shard_map/gvw,aptwgc->aptvgc/dot_general | solution.py:141
  178.3 52.9 %fusion.4 = f32[2,300,25,128,2]{3,4,2,1,0:T(2,128)} fusion(f32[2,300,25,3,128]{4,2,1,0,3:T(8,128)} %fusion.12, s32[3]{0:T(128)S(1)} %get-tuple-element.88), kind=kOutput, calls=%fused_computation.4 | convolution fusion | flops 138240000 | bytes 38400012 | tf_op jit(solution)/shard_map/gq,aptvgc->aptvqc/dot_general | solution.py:142
  231.2 13.0 copy.129
  246.2 174.9 %reduce-scatter.6.cloned.1.call-done = f32[1,2,300,25,128]{4,2,3,1,0:T(8,128)} async-done(((f32[1,2,300,25,256]{4,2,3,1,0:T(8,128)}), f32[1,2,300,25,128]{4,2,3,1,0:T(8,128)}) %reduce-scatter.6.cloned.1.call-update) | async-done | bytes 7680016 | tf_op jit(solution)/shard_map/reduce_scatter | solution.py:144
  426.3 30.0 %all-reduce.4 = (f32[128]{0:T(128)S(1)}, f32[]{:T(128)}) all-reduce(f32[128]{0:T(128)S(1)} %multiply_reduce_fusion.3, f32[]{:T(128)S(6)} %mul.274), channel_id=1, replica_groups=mesh['dp'=16,'sub'=2] {'dp'}, use_global_device_ids=true, to_apply=%region_5.6 | all-reduce | flops 129 | bytes 1032 | tf_op jit(solution)/shard_map/psum | solution.py:28
  462.3 33.2 %psum.89 = f32[128]{0:T(128)S(1)} all-reduce(f32[128]{0:T(128)S(1)} %multiply_reduce_fusion.2), channel_id=1, replica_groups=mesh['dp'=16,'sub'=2] {'dp'}, use_global_device_ids=true, to_apply=%region_9.10 | all-reduce | flops 128 | bytes 1024 | tf_op jit(solution)/shard_map/psum | solution.py:34
  504.8 92.4 %all-gather.6.cloned.1.call-done = bf16[1,2,300,25,256]{4,2,3,1,0:T(8,128)(2,1)} async-done(((bf16[1,2,300,25,128]{4,2,3,1,0:T(8,128)(2,1)}), bf16[1,2,300,25,256]{4,2,3,1,0:T(8,128)(2,1)}) %all-gather.6.cloned.1.call-update) | async-done | bytes 7680016 | tf_op jit(solution)/shard_map/all_gather | solution.py:149
  597.2 52.8 %pad_slice_fusion = (bf16[1,2,300,25,256]{4,2,3,1,0:T(8,128)(2,1)}, bf16[1,2,300,25,256]{4,2,3,1,0:T(8,128)(2,1)}, bf16[1,2,300,25,256]{4,2,3,1,0:T(8,128)(2,1)}...) fusion(bf16[1,2,300,25,256]{4,2,3,1,0:T(8,128)(2,1)} %all-gathe, ...), kind=kLoop, calls=%fused_computation.99 | loop fusion | bytes 69120000 | tf_op jit(solution)/shard_map/slice | solution.py:65
  650.0 10.3 copy.130
  660.3 12.9 reshape.466
  673.2 10.3 copy.131
  683.5 12.7 reshape.467
  696.3 10.3 copy.132
  706.5 12.8 reshape.468
  719.3 10.3 copy.133
  729.6 13.1 reshape.469
  742.7 10.3 copy.134
  753.0 12.7 reshape.470
  765.8 10.3 copy.135
  776.0 12.8 reshape.471
  788.8 10.3 copy.136
  799.1 12.9 reshape.472
  812.0 10.3 copy.137
  822.3 12.7 reshape.473
  835.0 10.3 copy.138
  845.3 13.1 reshape.474
  902.7 9.4 reshape.475
  912.1 29.5 %psum.90 = f32[128]{0:T(128)S(1)} all-reduce(f32[128]{0:T(128)S(1)} %get-tuple-element.86), channel_id=1, replica_groups=mesh['dp'=16,'sub'=2] {'dp'}, use_global_device_ids=true, to_apply=%region_11.12 | all-reduce | flops 128 | bytes 1024 | tf_op jit(solution)/shard_map/psum | solution.py:28
  950.1 33.1 %psum.91 = f32[128]{0:T(128)S(1)} all-reduce(f32[128]{0:T(128)S(1)} %multiply_reduce_fusion.4), channel_id=1, replica_groups=mesh['dp'=16,'sub'=2] {'dp'}, use_global_device_ids=true, to_apply=%region_13.14 | all-reduce | flops 128 | bytes 1024 | tf_op jit(solution)/shard_map/psum | solution.py:34
  983.9 16.6 fusion.212
  1000.4 29.6 %all-reduce.3 = (f32[128]{0:T(128)S(1)}, f32[128]{0:T(128)S(1)}) all-reduce(f32[128]{0:T(128)S(1)} %get-tuple-element.48, f32[128]{0:T(128)S(1)} %get-tuple-element.47), channel_id=1, replica_groups=mesh['dp'=16,'sub'=2] {'dp'}, use_global_device_ids=true, to_apply=%region_17.18 | all-reduce | flops 256 | bytes 2048 | tf_op jit(solution)/shard_map/psum | solution.py:41
  1030.1 10.3 multiply_convert_fusion.1
  1040.4 11.9 pad_slice_fusion.8
  1066.8 9.8 fusion.178
  1174.7 8.9 convolution_add_fusion.7
  1191.2 8.9 convolution_add_fusion.5
  1207.8 8.9 convolution_add_fusion.3
  1224.5 8.9 convolution_add_fusion.1
  1241.0 17.6 reshape.485
  1258.5 17.3 copy.151
  1275.9 173.0 %reduce-scatter.8.cloned.1.call-done = f32[1,2,300,25,128]{4,2,3,1,0:T(8,128)} async-done(((f32[1,2,300,25,256]{4,2,3,1,0:T(8,128)}), f32[1,2,300,25,128]{4,2,3,1,0:T(8,128)}) %reduce-scatter.8.cloned.1.call-update) | async-done | bytes 7680016 | tf_op jit(solution)/shard_map/reduce_scatter | solution.py:165
  1448.9 12.2 fusion.211
  1461.1 29.5 %all-reduce.2 = (f32[128]{0:T(128)S(1)}, f32[128]{0:T(128)S(1)}) all-reduce(f32[128]{0:T(128)S(1)} %get-tuple-element.46, f32[128]{0:T(128)S(1)} %get-tuple-element.45), channel_id=1, replica_groups=mesh['dp'=16,'sub'=2] {'dp'}, use_global_device_ids=true, to_apply=%region_22.23 | all-reduce | flops 256 | bytes 2048 | tf_op jit(solution)/shard_map/psum | solution.py:41
  1490.6 8.6 multiply_convert_fusion
  1499.3 11.6 copy.157
  1510.9 12.9 reshape.489
  1559.9 36.6 %all-gather.8.cloned.1.call-done = bf16[1,2,300,25,256]{4,2,3,1,0:T(8,128)(2,1)} async-done(((bf16[1,2,300,25,128]{4,2,3,1,0:T(8,128)(2,1)}), bf16[1,2,300,25,256]{4,2,3,1,0:T(8,128)(2,1)}) %all-gather.8.cloned.1.call-update) | async-done | bytes 7680016 | tf_op jit(solution)/shard_map/all_gather | solution.py:170
  1596.5 14.4 reshape.486
  1610.9 15.3 convolution_bitcast_fusion
  1626.2 35.9 %convert_bitcast_fusion = bf16[1,2,300,25,3,128]{5,3,2,1,4,0:T(8,128)(2,1)} fusion(f32[3,25,25,1,1]{1,2,4,3,0:T(8,128)S(1)} %copy-done.14, f32[2,300,25,3,128]{4,3,2,1,0:T(4,128)} %convolution_bitcast_fusion), kind=kOutput, calls=%fused_computation.26 | convolution fusion | flops 1733760000 | bytes 34567500 | tf_op jit(solution)/shard_map/gvw,aptvgc->aptwgc/dot_general | solution.py:178
  1662.1 17.1 copy.156
  1686.8 17.2 copy.155
  1704.0 22.5 %dot_general.154 = bf16[2,300,25,384]{3,1,2,0:T(8,128)(2,1)} reshape(bf16[1,2,300,25,3,128]{5,4,2,3,1,0:T(4,128)(2,1)} %copy.155) | data formatting | bytes 23040000 | tf_op jit(solution)/shard_map/dot_general | solution.py:185
  1726.6 11.7 convert_bitcast_fusion.1
  1738.3 15.8 copy.188
  1754.1 18.9 reshape.519
  1773.1 10.3 copy.161
  1783.5 39.9 %fusion.156 = f32[3,25,25]{2,1,0:T(8,128)S(1)} fusion(f32[2,300,25,3,128]{4,1,3,2,0:T(8,128)} %fusion.32, f32[2,300,25,3,128]{4,3,2,1,0:T(4,128)} %convolution_bitcast_fusion), kind=kOutput, calls=%fused_computation.128 | convolution fusion | flops 1728000000 | bytes 46087500 | tf_op jit(solution)/shard_map/aptvgc,aptwgc->gvw/dot_general | solution.py:179
  1823.6 40.6 %psum.97 = f32[3,25,25]{2,0,1:T(4,128)S(1)} all-reduce(f32[3,25,25]{2,0,1:T(4,128)S(1)} %convolution_multiply_fusion), channel_id=1, replica_groups=mesh['dp'=16,'sub'=2] {'dp','sub'}, use_global_device_ids=true, to_apply=%region_25.26 | all-reduce | flops 1875 | bytes 15000 | tf_op jit(solution)/shard_map/psum | solution.py:196
  1866.8 11.2 reduce-scatter.10.cloned.1.call-done
  1877.9 13.0 reshape.520
  1907.1 10.4 copy.162
  (205 shorter events, 288.0 us)
Async XLA Ops:
  7.2 4.8 copy-start.34
  7.2 5.6 copy-start.44
  7.2 5.9 copy-start.10
  7.2 104.0 %all-gather.4.cloned.1.call-start = ((), (), s32[]{:S(2)}) async-start(), calls=%async_computation.3 | async-start | bytes 11673600 | tf_op jit(solution)/shard_map/all_gather | solution.py:138
  11.8 409.2 %reduce-scatter.6.cloned.1.call-start = ((), (), s32[]{:S(2)}) async-start(), calls=%async_computation.4 | async-start | bytes 23347200 | tf_op jit(solution)/shard_map/reduce_scatter | solution.py:144
  11.9 1.1 copy-start.46
  12.0 166.4 %copy-start.35 = (s32[3]{0:T(128)}, s32[3]{0:T(128)S(1)}, u32[]{:S(2)}) copy-start(s32[3]{0:T(128)S(1)} %get-tuple-element.88) | copy-start | bytes 40
  12.0 0.6 copy-start.22
  12.1 0.6 copy-start.18
  12.2 0.8 copy-start.42
  13.1 111.8 %copy-start.13 = (f32[3,25,25,1,1]{1,2,4,3,0:T(8,128)}, f32[3,25,25,1,1]{1,2,4,3,0:T(8,128)S(1)}, u32[]{:S(2)}) copy-start(f32[3,25,25,1,1]{1,2,4,3,0:T(8,128)S(1)} %copy.171) | copy-start | bytes 22504
  244.2 0.7 copy-start.45
  244.2 353.0 %all-gather.6.cloned.1.call-start = ((), (), s32[]{:S(2)}) async-start(), calls=%async_computation.5 | async-start | bytes 11673600 | tf_op jit(solution)/shard_map/all_gather | solution.py:149
  246.1 257.7 %copy-start.15 = (f32[2]{0:T(128)}, f32[2]{0:T(128)S(1)}, u32[]{:S(2)}) copy-start(f32[2]{0:T(128)S(1)} %convert_bitcast_fusion.2) | copy-start | bytes 28
  246.1 249.4 %copy-start.28 = (f32[128]{0:T(128)S(1)}, f32[128]{0:T(128)}, u32[]{:S(2)}) copy-start(f32[128]{0:T(128)} %param.16) | copy-start | bytes 1540
  246.1 250.5 %copy-start.31 = (f32[128]{0:T(128)S(1)}, f32[128]{0:T(128)}, u32[]{:S(2)}) copy-start(f32[128]{0:T(128)} %param.17) | copy-start | bytes 1540
  457.0 46.6 %copy-start.24 = (f32[128]{0:T(128)}, f32[128]{0:T(128)S(1)}, u32[]{:S(2)}) copy-start(f32[128]{0:T(128)S(1)} %broadcast_divide_fusion.1) | copy-start | bytes 1540
  496.7 6.9 copy-start.26
  503.6 945.3 %reduce-scatter.8.cloned.1.call-start = ((), (), s32[]{:S(2)}) async-start(), calls=%async_computation.6 | async-start | bytes 23347200 | tf_op jit(solution)/shard_map/reduce_scatter | solution.py:165
  845.3 18.6 slice-start.2
  858.4 5.5 slice-start.3
  858.4 8.7 slice-start.4
  863.9 3.2 slice-start.5
  867.1 3.2 copy-start.7
  867.2 8.7 slice-start.6
  870.3 5.5 slice-start.7
  883.9 11.0 slice-start
  889.4 5.5 slice-start.1
  889.4 5.5 copy-start.12
  902.7 80.5 %copy-start.33 = (f32[128]{0:T(128)S(1)}, f32[128]{0:T(128)}, u32[]{:S(2)}) copy-start(f32[128]{0:T(128)} %param.19) | copy-start | bytes 1540
  902.7 81.2 %copy-start.41 = (f32[128]{0:T(128)S(1)}, f32[128]{0:T(128)}, u32[]{:S(2)}) copy-start(f32[128]{0:T(128)} %param.20) | copy-start | bytes 1540
  983.9 46.2 %copy-start.16 = (f32[2]{0:T(128)S(1)}, f32[2]{0:T(128)}, u32[]{:S(2)}) copy-start(f32[2]{0:T(128)} %copy-done.15) | copy-start | bytes 28
  1030.1 10.3 copy-start.37
  1030.1 10.3 copy-start.38
  1040.4 11.9 copy-start
  1066.8 9.8 copy-start.6
  1174.7 8.9 copy-start.2
  1191.2 8.9 copy-start.3
  1207.8 8.9 copy-start.4
  1224.5 8.9 copy-start.5
  1275.8 173.1 %copy-start.25 = (f32[128]{0:T(128)S(1)}, f32[128]{0:T(128)}, u32[]{:S(2)}) copy-start(f32[128]{0:T(128)} %copy-done.24) | copy-start | bytes 1540
  1275.8 173.1 %copy-start.27 = (f32[128]{0:T(128)S(1)}, f32[128]{0:T(128)}, u32[]{:S(2)}) copy-start(f32[128]{0:T(128)} %copy-done.26) | copy-start | bytes 1540
  1275.8 173.1 %copy-start.29 = (f32[128]{0:T(128)S(1)}, f32[128]{0:T(128)}, u32[]{:S(2)}) copy-start(f32[128]{0:T(128)} %param.16) | copy-start | bytes 1540
  1275.8 173.1 %copy-start.32 = (f32[128]{0:T(128)S(1)}, f32[128]{0:T(128)}, u32[]{:S(2)}) copy-start(f32[128]{0:T(128)} %param.17) | copy-start | bytes 1540
  1275.8 214.8 %copy-start.17 = (f32[2]{0:T(128)S(1)}, f32[2]{0:T(128)}, u32[]{:S(2)}) copy-start(f32[2]{0:T(128)} %copy-done.15) | copy-start | bytes 28
  1275.9 214.8 %copy-start.30 = (f32[128]{0:T(128)S(1)}, f32[128]{0:T(128)}, u32[]{:S(2)}) copy-start(f32[128]{0:T(128)} %get-tuple-element.57) | copy-start | bytes 1540
  1275.9 320.7 %all-gather.8.cloned.1.call-start = ((), (), s32[]{:S(2)}) async-start(), calls=%async_computation.7 | async-start | bytes 11673600 | tf_op jit(solution)/shard_map/all_gather | solution.py:170
  1490.6 8.6 copy-start.39
  1490.6 8.6 copy-start.40
  1499.3 365.6 %all-reduce.8.cloned.1.call-start = ((), (), s32[]{:S(2)}) async-start(), calls=%async_computation.9 | async-start | bytes 3145728 | tf_op jit(solution)/shard_map/psum | solution.py:195
  1523.8 7.2 copy-start.1
  1531.1 12.2 slice-start.8
  1537.2 6.1 slice-start.9
  1559.9 66.3 %copy-start.9 = (f32[9,256,128]{2,1,0:T(8,128)}, f32[9,256,128]{2,1,0:T(8,128)S(1)}, u32[]{:S(2)}) copy-start(f32[9,256,128]{2,1,0:T(8,128)S(1)} %fusion.151) | copy-start | bytes 3538948
  1559.9 51.0 %copy-start.36 = (s32[3]{0:T(128)S(1)}, s32[3]{0:T(128)}, u32[]{:S(2)}) copy-start(s32[3]{0:T(128)} %copy-done.35) | copy-start | bytes 40
  1610.9 15.3 copy-start.14
  1686.8 191.2 %reduce-scatter.10.cloned.1.call-start = ((), (), s32[]{:S(2)}) async-start(), calls=%async_computation.8 | async-start | bytes 11599872
  1704.0 22.5 %copy-start.11 = (bf16[256,384]{1,0:T(8,128)(2,1)S(1)}, bf16[256,384]{1,0:T(8,128)(2,1)}, u32[]{:S(2)}) copy-start(bf16[256,384]{1,0:T(8,128)(2,1)} %param.14) | copy-start | bytes 589828
  1783.4 39.9 %copy-start.19 = (f32[1,25,25]{2,0,1:T(1,128)S(1)}, f32[1,25,25]{2,0,1:T(1,128)}, u32[]{:S(2)}) copy-start(f32[1,25,25]{2,0,1:T(1,128)} %copy-done.18) | copy-start | bytes 7504
  1783.4 39.9 %copy-start.21 = (f32[1,25,25]{2,0,1:T(1,128)S(1)}, f32[1,25,25]{2,0,1:T(1,128)}, u32[]{:S(2)}) copy-start(f32[1,25,25]{2,0,1:T(1,128)} %copy-done.20) | copy-start | bytes 7504
  1783.4 39.9 %copy-start.23 = (f32[1,25,25]{2,0,1:T(1,128)S(1)}, f32[1,25,25]{2,0,1:T(1,128)}, u32[]{:S(2)}) copy-start(f32[1,25,25]{2,0,1:T(1,128)} %copy-done.22) | copy-start | bytes 7504
  1783.5 39.9 %copy-start.43 = (f32[25]{0:T(128)S(1)}, f32[25]{0:T(128)}, u32[]{:S(2)}) copy-start(f32[25]{0:T(128)} %copy-done.42) | copy-start | bytes 304
  1783.5 39.9 %copy-start.47 = (s32[3]{0:T(128)S(1)}, s32[3]{0:T(128)}, u32[]{:S(2)}) copy-start(s32[3]{0:T(128)} %copy-done.46) | copy-start | bytes 40
  1907.1 10.4 copy-start.8
  (1 other events, 0.6 us)
Sparse Core Ops, SparseCore 0:
  12.0 99.2 all-gather.3
  244.4 176.6 reduce-scatter.5
  503.7 93.4 all-gather.5
  1276.0 172.9 reduce-scatter.7
  1499.4 97.0 all-gather.7
  1686.9 94.6 all-reduce.7
  1783.9 94.0 reduce-scatter.9
where the time goes:
time: 1940 us; the launch traced here: 1930 us
  local copies, waits for them, and re-layouts  626 us (32%)
  waiting for transfers between devices  586 us (30%)
  matrix products  387 us (20%)
  blocking collectives  226 us (12%)
  other arithmetic  84.9 us (4%)
    reshape x19, local copies, waits for them, and re-layouts, flatten_rows(): return values.reshape(-1, values.shape[-1])  198 us
    reduce_scatter x1, waiting for transfers between devices, local(): summed = lax.psum_scatter(term, 'sub', scatter_dimension=4, tiled=True)  175 us
    reduce_scatter x1, waiting for transfers between devices, local(): lax.psum_scatter(grad_activity_full, 'sub', scatter_dimension=4, tiled=True)  173 us
    slice x9, local copies, waits for them, and re-layouts, temporal(): window = padded[:, :, tap_index:tap_index + frames]  135 us
    all_gather x1, waiting for transfers between devices, local(): whole_inputs = lax.all_gather(features, 'sub', axis=4, tiled=True)  97.9 us
    all_gather x1, waiting for transfers between devices, local(): whole_activity = lax.all_gather(activity, 'sub', axis=4, tiled=True)  92.4 us
    unnamed x127, local copies, waits for them, and re-layouts  86.4 us
    dot_general x9, matrix products, temporal_input_grad(): lax.dot_general(flatten_rows(window), weights[tap_index], column_contract...  76.1 us
  transfers between devices with their start and end apart: 7, of which 6 were waited for; matrix products, arithmetic and copies ran while one was open for 10% of the time, Pallas kernels for 0%

commit v1 on v0

v1 whole, which is shorter than its diff:
```python
import functools

import jax
import jax.numpy as jnp
from jax import lax
from jax.experimental import pallas as pl
from jax.experimental.pallas import tpu as pltpu
from jax.sharding import PartitionSpec as P

norm_eps = 1e-05
exact_mode = lax.Precision.HIGHEST
MESH = pl.DeviceIdType.MESH
TAPS = 9
HALO = TAPS // 2
NB = 8
RW = 2 * NB
G = 4
tanh_scale = 0.7978845608028654
tanh_cubic = 0.044715


def gelu(x):
    t = jnp.tanh(tanh_scale * (x + tanh_cubic * x * x * x))
    return 0.5 * x * (1.0 + t)


def gelu_both(x):
    x2 = x * x
    t = jnp.tanh(tanh_scale * x * (1.0 + tanh_cubic * x2))
    h = 0.5 * (1.0 + t)
    slope = h + 0.5 * x * (1.0 - t * t) * (tanh_scale + (3.0 * tanh_scale * tanh_cubic) * x2)
    return x * h, slope


class Sizes:
    def __init__(self, n_dp, frames, joints, half):
        self.n_dp, self.frames, self.joints, self.half = n_dp, frames, joints, half
        self.chan = 2 * half
        self.blk = -(-frames // (2 * NB))
        self.win = self.blk * NB
        self.pad = 2 * self.win - frames
        self.rows = joints * RW
        self.total = self.blk * self.rows
        self.chips = n_dp // 2
        self.p1 = min(8, self.chips)
        self.p2 = self.chips // self.p1
        cut = self.blk - self.pad
        step = -(-cut // 3)
        self.chunks = [(a, min(a + step, cut)) for a in range(0, cut, step)]
        if self.pad:
            self.chunks.append((cut, self.blk))
        self.locals = [(0, cut)] + ([(cut, self.blk)] if self.pad else [])


def mega(
    z,
    feat,
    cot,
    wt_in,
    ws_in,
    imp,
    par,
    pres,
    g1,
    b1,
    g2,
    b2,
    act_own,
    act_rcv,
    ing_own,
    ing_rcv,
    tg_out,
    sg_out,
    sums_out,
    ig_out,
    xh,
    ct,
    wt,
    ws,
    parts,
    chain,
    mixed,
    summed,
    acth,
    conv,
    gch,
    zz,
    iz,
    gb,
    gb_core,
    gb_low,
    gb_chips,
    gb_far,
    gb_sum,
    gb_pair,
    gb_all,
    sg,
    prm,
    adj,
    edge,
    kin,
    halo_s,
    halo_r,
    arA,
    arB,
    arC,
    sem_l,
    sem_f,
    sem_c,
    sem_a,
    sem_i,
    sem_w,
    sem_h,
    sem_g,
    semA,
    semB,
    semC,
):
    f32, bf = jnp.float32, jnp.bfloat16
    J, C, H, L, R = z.joints, z.chan, z.half, z.blk, z.rows
    s = lax.axis_index("sub")
    dp = lax.axis_index("dp")
    o = 1 - s
    core = lax.rem(dp, 2)
    chip = lax.div(dp, 2)
    c1 = lax.rem(chip, z.p1)
    c2 = lax.div(chip, z.p1)
    partner = (dp, o)

    def peer_a(t):
        return (2 * chip + lax.div(t, 2), lax.rem(t, 2))

    def peer_b(t):
        return (2 * (c2 * z.p1 + t) + core, s)

    def peer_c(t):
        return (2 * (t * z.p1 + c1) + core, s)

    def remote(src, dst, ssem, rsem, dev):
        return pltpu.make_async_remote_copy(
            src_ref=src,
            dst_ref=dst,
            send_sem=ssem,
            recv_sem=rsem,
            device_id=dev,
            device_id_type=MESH,
        )

    def frame_row(w, b, a0, a1):
        at = w * z.win + (b * L + a0)
        if b == NB - 1 and z.pad and a0 >= L - z.pad:
            at = at - w * z.pad
        return at

    local = []
    for which, (src, dst) in enumerate(((feat, xh), (cot, ct))):
        for i, (a0, a1) in enumerate(z.locals):
            for b in range(NB):
                cp = pltpu.make_async_copy(
                    src.at[pl.ds(frame_row(s, b, a0, a1), a1 - a0)],
                    dst.at[s, pl.ds(a0, a1 - a0), :, b],
                    sem_l.at[which, i * NB + b],
                )
                cp.start()
                local.append(cp)
    lw = [
        pltpu.make_async_copy(ws_in, ws.at[:, pl.ds(pl.multiple_of(s * 3 * H, H), 3 * H)], sem_l.at[2, 0]),
        pltpu.make_async_copy(wt_in, wt.at[:, :, pl.ds(pl.multiple_of(s * H, H), H)], sem_l.at[2, 1]),
    ]
    for cp in lw:
        cp.start()
    for i, v in enumerate((g1, b1, g2, b2)):
        prm[s, i : i + 1] = v[...]

    bar = pltpu.get_barrier_semaphore()
    qa = core * 2 + s
    n_peers = 0
    for d in range(1, 4):
        pl.semaphore_signal(bar, inc=1, device_id=peer_a(lax.rem(qa + d, 4)), device_id_type=MESH)
        n_peers += 1
    for d in range(1, z.p1):
        pl.semaphore_signal(bar, inc=1, device_id=peer_b(lax.rem(c1 + d, z.p1)), device_id_type=MESH)
        n_peers += 1
    for d in range(1, z.p2):
        pl.semaphore_signal(bar, inc=1, device_id=peer_c(lax.rem(c2 + d, z.p2)), device_id_type=MESH)
        n_peers += 1
    with jax.named_scope("barrier"):
        pl.semaphore_wait(bar, n_peers)

    slice_rows = H // z.p1
    row0 = pl.multiple_of(core * H + c1 * slice_rows, slice_rows)

    def ws_at(half, r0, n):
        return ws.at[pl.ds(r0, n), pl.ds(pl.multiple_of(half * 3 * H, H), 3 * H)]

    def wt_at(half, r0, n):
        return wt.at[:, pl.ds(r0, n), pl.ds(pl.multiple_of(half * H, H), H)]

    sends = []

    def go(cp):
        cp.start()
        sends.append(cp)
        return cp

    def arrive(dst, rsem):
        remote(dst, dst, rsem, rsem, partner).wait_recv()

    go(remote(prm.at[s], prm.at[s], sem_w.at[0, 0], sem_w.at[1, 0], partner))
    go(remote(ws_in.at[pl.ds(row0, slice_rows)], ws_at(s, row0, slice_rows), sem_w.at[0, 1], sem_w.at[1, 1], partner))
    go(remote(wt_in.at[:, pl.ds(row0, slice_rows)], wt_at(s, row0, slice_rows), sem_w.at[0, 2], sem_w.at[1, 2], partner))

    def send_rows(src, dst, sem, j):
        a0, a1 = z.chunks[j]
        for b in range(NB):
            go(
                remote(
                    src.at[pl.ds(frame_row(o, b, a0, a1), a1 - a0)],
                    dst.at[s, pl.ds(a0, a1 - a0), :, b],
                    sem.at[0, j, b],
                    sem.at[1, j, b],
                    partner,
                )
            )

    def take_rows(dst, sem, j):
        a0, a1 = z.chunks[j]
        for b in range(NB):
            arrive(dst.at[o, pl.ds(a0, a1 - a0), :, b], sem.at[1, j, b])

    n_chunks = len(z.chunks)
    for j in range(n_chunks):
        send_rows(feat, xh, sem_f, j)

    ri = lax.broadcasted_iota(jnp.int32, (J, J), 0)
    ci = lax.broadcasted_iota(jnp.int32, (J, J), 1)
    eye = jnp.where(ri == ci, 1.0, 0.0).astype(f32)
    up = jnp.zeros((J, J), f32)
    down = jnp.zeros((J, J), f32)
    for v in range(1, J):
        pv = par[v]
        up = jnp.where((ri == v) & (ci == pv), 1.0, up)
        down = jnp.where((ci == v) & (ri == pv), 1.0, down)
    degree = jnp.sum(eye + up + down, axis=0, keepdims=True)
    adjacent = [eye / degree, up / degree, down / degree]
    mixing = [adjacent[k] * imp[k] for k in range(3)]
    for k in range(3):
        adj[k] = adjacent[k]
    last = (((1,), (1,)), ((), ()))
    first = (((0,), (0,)), ((), ()))
    wide = jnp.ones((J, C), f32)
    edge[0] = jnp.dot(mixing[0], wide, precision=exact_mode, preferred_element_type=f32)
    edge[1] = jnp.dot(mixing[1], wide, precision=exact_mode, preferred_element_type=f32)
    edge[2] = lax.dot_general(mixing[2], wide, first, precision=exact_mode, preferred_element_type=f32)

    def kin_body(v, _):
        pv = par[v]
        sibling = jnp.int32(0)
        child = jnp.int32(0)
        for w in range(J - 1, 0, -1):
            pw_ = par[w]
            sibling = jnp.where((pw_ == pv) & (w > v), w, sibling)
            child = jnp.where(pw_ == v, w, child)
        kin[0, v] = sibling
        kin[1, v] = child
        return 0

    lax.fori_loop(0, J, kin_body, 0)
    chain[0] = jnp.zeros((RW, C), f32)

    for i, at in ((0, ws_at), (1, wt_at)):
        arrive(at(o, row0, slice_rows), sem_w.at[1, 1 + i])
        for d in range(1, z.p1):
            t = lax.rem(c1 + d, z.p1)
            go(
                remote(
                    at(o, row0, slice_rows),
                    at(o, row0, slice_rows),
                    sem_w.at[0, 4 + i * 16 + d],
                    sem_w.at[1, 4 + i * 16 + d],
                    peer_b(t),
                )
            )
    for i, at in ((0, ws_at), (1, wt_at)):
        for d in range(1, z.p1):
            t = lax.rem(c1 + z.p1 - d, z.p1)
            arrive(
                at(o, pl.multiple_of(core * H + t * slice_rows, slice_rows), slice_rows),
                sem_w.at[1, 4 + i * 16 + d],
            )
        mine = pl.multiple_of(core * H, H)
        go(remote(at(o, mine, H), at(o, mine, H), sem_w.at[0, 36 + i], sem_w.at[1, 36 + i], (2 * chip + 1 - core, s)))
    theirs = pl.multiple_of((1 - core) * H, H)
    arrive(ws_at(o, theirs, H), sem_w.at[1, 36])
    for cp in lw:
        cp.wait()
    arrive(prm.at[o], sem_w.at[1, 0])
    p0 = pres[0, 0].astype(f32)
    p1 = pres[0, 1].astype(f32)
    ri16 = lax.broadcasted_iota(jnp.int32, (RW, C), 0)
    pw = jnp.where((ri16 & 1) == 0, p0, p1).astype(f32)
    tail = jnp.where(ri16 >= RW - 2, 1.0, 0.0).astype(f32)
    side = s.astype(f32)

    def real(a):
        late = jnp.where(a >= L - z.pad, side, 0.0) if z.pad else 0.0
        return 1.0 - tail * late

    def tiles(x):
        return x.reshape(-1, RW, C)

    def times(x, m):
        return (tiles(x) * m[None]).reshape(x.shape)

    def down_rows(x):
        return jnp.sum(tiles(x), axis=0)

    def row_sum(x):
        return jnp.sum(x, axis=0, keepdims=True)

    def param(i):
        return jnp.concatenate([prm[0, i : i + 1], prm[1, i : i + 1]], axis=1)

    def whole(ref, a):
        return jnp.concatenate([ref[0, a].reshape(R, H), ref[1, a].reshape(R, H)], axis=1)

    def put(ref, a, value):
        for h in range(2):
            ref[h, a] = value[:, h * H : (h + 1) * H].reshape(J, NB, 2, H)

    def spread(buf, sem, r, q, n, peer, val):
        buf[r, q] = val
        for d in range(1, n):
            go(remote(buf.at[r, q], buf.at[r, q], sem.at[0, r, d], sem.at[1, r, d], peer(lax.rem(q + d, n))))

    def gather(buf, sem, r, q, n):
        for d in range(1, n):
            arrive(buf.at[r, lax.rem(q + n - d, n)], sem.at[1, r, d])
        return [buf[r, i] for i in range(n)]

    def add_up(parts):
        t = parts[0]
        for x in parts[1:]:
            t = t + x
        return t

    def merge(parts):
        n = add_up([x[0:1] for x in parts])
        below = jnp.maximum(n, 1.0)
        mean = add_up([x[0:1] * x[1:2] for x in parts]) / below
        spread_up = add_up([x[2:3] + x[0:1] * (x[1:2] - mean) * (x[1:2] - mean) for x in parts])
        return jnp.concatenate([n, mean, spread_up, jnp.zeros((5, C), f32)], axis=0)

    def all_start(r, val):
        spread(arA, semA, r, qa, 4, peer_a, val)

    def all_next(r, join):
        val = join(gather(arA, semA, r, qa, 4))
        if z.p1 > 1:
            spread(arB, semB, r, c1, z.p1, peer_b, val)
        else:
            arB[r, 0] = val

    def all_end(r, join):
        val = join(gather(arB, semB, r, c1, z.p1))
        if z.p2 > 1:
            spread(arC, semC, r, c2, z.p2, peer_c, val)
            val = join(gather(arC, semC, r, c2, z.p2))
        return val

    def moments(val_k, s1, s2):
        n = (p0 + p1) * (z.win - z.pad * side) * J
        below = jnp.maximum(n, 1.0)
        s1, s2 = row_sum(s1), row_sum(s2)
        return jnp.concatenate(
            [jnp.zeros((1, C), f32) + n, val_k + s1 / below, s2 - s1 * s1 / below, jnp.zeros((5, C), f32)], axis=0
        )

    zero16 = jnp.zeros((RW, C), f32)
    zero1 = jnp.zeros((1, C), f32)

    def link(value, k):
        for v in range(J - 1, 0, -1):
            chain[v] = value(v) * edge[k, v : v + 1] + chain[kin[0, v]]

    def spatial_body(a, carry):
        k_shift, s1, s2 = carry
        f = whole(xh, a)
        for k in range(3):
            parts[k] = jnp.dot(f, ws[:, k * C : (k + 1) * C], preferred_element_type=f32).reshape(J, RW, C)
        link(lambda v: parts[2, v], 2)
        for v in range(J):
            t = parts[0, v] * edge[0, v : v + 1] + chain[kin[1, v]]
            if v:
                t = t + parts[1, par[v]] * edge[1, v : v + 1]
            summed[a, v] = t
        t = summed[a].reshape(R, C)
        k_shift = jnp.where(a == 0, row_sum(t) * (1.0 / R), k_shift)
        w = pw * real(a)
        d = tiles(t - k_shift)
        wd = d * w[None]
        return k_shift, s1 + jnp.sum(wd, axis=0), s2 + jnp.sum(wd * d, axis=0)

    carry = (zero1, zero16, zero16)
    n_local = len(z.locals) * NB
    for cp in local[:n_local]:
        cp.wait()
    for j, (a0, a1) in enumerate(z.chunks):
        with jax.named_scope("features_wait"):
            take_rows(xh, sem_f, j)
        if j == n_chunks - 1:
            for i in range(n_chunks):
                send_rows(cot, ct, sem_c, i)
        with jax.named_scope("spatial"):
            carry = lax.fori_loop(a0, a1, spatial_body, carry)

    lane = lax.broadcasted_iota(jnp.int32, (64, R), 1)
    line = lax.broadcasted_iota(jnp.int32, (64, R), 0)
    off = (RW - 2) * o
    pick = jnp.where(
        (lane == lax.shift_right_logical(line, 1) * RW + off + (line & 1)) & (line < 2 * J), 1.0, 0.0
    ).astype(bf)
    edge_a = (L - HALO) * o

    def halo_out(ref, slot, i):
        for h in range(HALO):
            halo_s[slot, h] = jnp.dot(pick, ref(edge_a + h).astype(bf), preferred_element_type=f32).astype(bf)
        go(remote(halo_s.at[slot], halo_r.at[slot], sem_h.at[0, i], sem_h.at[1, i], partner))

    def halo_in(slot, i):
        arrive(halo_r.at[slot], sem_h.at[1, i])

    row_in = lax.broadcasted_iota(jnp.int32, (R, C), 0) & (RW - 1)
    fside = 1.0 - side

    def fill_halo(buf, fresh):
        for h in range(HALO):
            extra = lax.dot_general(pick, fresh(h), first, preferred_element_type=f32)
            lower = pltpu.roll(buf[L + h].reshape(R, C).astype(f32), 2, 0)
            lower = jnp.where(row_in < 2, extra * side, lower)
            buf[h] = tiles(lower.astype(bf))
            upper = pltpu.roll(buf[HALO + h].reshape(R, C).astype(f32), R - 2, 0)
            upper = jnp.where(row_in >= RW - 2, extra * fside, upper)
            buf[HALO + L + h] = tiles(upper.astype(bf))

    halo_out(lambda a: summed[a].reshape(R, C), 0, 0)
    all_start(0, moments(*carry))
    with jax.named_scope("st1"):
        all_next(0, merge)
        st1 = all_end(0, merge)
    count = jnp.maximum(st1[0:1], 1.0)
    mean1 = st1[1:2]
    rstd1 = lax.rsqrt(st1[2:3] / count + norm_eps)
    gain1, shift1 = param(0), param(1)
    scale1 = rstd1 * gain1

    def act_body(a, _):
        t = gelu((summed[a].reshape(R, C) - mean1) * scale1 + shift1)
        acth[a + HALO] = tiles(times(t, real(a)).astype(bf))
        return 0

    with jax.named_scope("act"):
        lax.fori_loop(0, L, act_body, 0)
    halo_in(0, 0)
    fill_halo(acth, lambda h: gelu((halo_r[0, h].astype(f32) - mean1) * scale1 + shift1).astype(bf))

    arrive(wt_at(o, theirs, H), sem_w.at[1, 37])

    def conv_block(a0, n, carry):
        k_shift, s1, s2 = carry
        t = jnp.zeros((n * R, C), f32)
        for tap in range(TAPS):
            t = t + jnp.dot(acth[pl.ds(a0 + tap, n)].reshape(n * R, C), wt[tap], preferred_element_type=f32)
        conv[pl.ds(a0, n)] = t.reshape(n, R, C)
        k_shift = jnp.where(a0 == 0, row_sum(t[:R]) * (1.0 / R), k_shift)
        for i in range(n):
            w = pw * real(a0 + i)
            d = tiles(t[i * R : (i + 1) * R] - k_shift)
            wd = d * w[None]
            s1 = s1 + jnp.sum(wd, axis=0)
            s2 = s2 + jnp.sum(wd * d, axis=0)
        return k_shift, s1, s2

    def blocks(fun, carry):
        carry = lax.fori_loop(0, L // G, lambda i, c: fun(i * G, G, c), carry)
        if L % G:
            carry = fun(L // G * G, L % G, carry)
        return carry

    with jax.named_scope("conv"):
        carry = blocks(conv_block, (zero1, zero16, zero16))
    all_start(1, moments(*carry))
    with jax.named_scope("st2"):
        all_next(1, merge)
        st2 = all_end(1, merge)
    mean2 = st2[1:2]
    rstd2 = lax.rsqrt(st2[2:3] / count + norm_eps)
    gain2, shift2 = param(2), param(3)

    for cp in local[n_local:]:
        cp.wait()

    def out_body(a, carry):
        sa, sb = carry
        normed = (conv[a] - mean2) * rstd2
        level = normed * gain2 + shift2 + whole(xh, a).astype(f32)
        value, slope = gelu_both(level)
        put(zz, a, value.astype(bf))
        gp = whole(ct, a).astype(f32) * slope
        conv[a] = gp
        put(ct, a, normed.astype(bf))
        gm = tiles(gp) * real(a)[None]
        return sa + jnp.sum(gm, axis=0), sb + jnp.sum(gm * tiles(normed), axis=0)

    carry = (zero16, zero16)
    outs = []

    def ship(buf, own, rcv, sem, j):
        a0, a1 = z.chunks[j]
        at = pl.ds(a0, a1 - a0)
        go(remote(buf.at[o, at], rcv.at[at], sem.at[0, j], sem.at[1, j], partner))
        cp = pltpu.make_async_copy(buf.at[s, at], own.at[at], sem.at[2, j])
        cp.start()
        outs.append(cp)

    for j, (a0, a1) in enumerate(z.chunks):
        with jax.named_scope("cotangent_wait"):
            take_rows(ct, sem_c, j)
        with jax.named_scope("level_two"):
            carry = lax.fori_loop(a0, a1, out_body, carry)
        ship(zz, act_own, act_rcv, sem_a, j)

    halo_out(lambda a: conv[a], 1, 1)
    halo_out(lambda a: whole(ct, a), 2, 2)
    pad6 = jnp.zeros((6, C), f32)
    all_start(2, jnp.concatenate([row_sum(carry[0]), row_sum(carry[1]), pad6], axis=0))
    with jax.named_scope("sum2"):
        all_next(2, add_up)
        sum2 = all_end(2, add_up)
    out_scale = gain2 * rstd2
    out_shift = out_scale * sum2[0:1] / count
    out_slope = out_scale * sum2[1:2] / count

    def back(grad, x, scale, shift, slope):
        corr = tiles(x * slope + shift) * pw[None]
        return grad * scale - corr.reshape(grad.shape)

    def gconv_body(a, _):
        gp = conv[a]
        t = back(gp, whole(ct, a).astype(f32), out_scale, out_shift, out_slope)
        gch[a + HALO] = tiles(times(t, real(a)).astype(bf))
        put(ct, a, gp.astype(bf))
        return 0

    with jax.named_scope("gconv"):
        lax.fori_loop(0, L, gconv_body, 0)
    halo_in(1, 1)
    halo_in(2, 2)
    fill_halo(
        gch,
        lambda h: back(halo_r[1, h].astype(f32), halo_r[2, h].astype(f32), out_scale, out_shift, out_slope).astype(bf),
    )

    def gact_block(a0, n, carry):
        sa, sb = carry
        t = jnp.zeros((n * R, C), f32)
        for tap in range(TAPS):
            t = t + lax.dot_general(
                gch[pl.ds(a0 + TAPS - 1 - tap, n)].reshape(n * R, C), wt[tap], last, preferred_element_type=f32
            )
        for i in range(n):
            centred = summed[a0 + i].reshape(R, C) - mean1
            _, slope = gelu_both(centred * scale1 + shift1)
            gl = t[i * R : (i + 1) * R] * slope
            conv[a0 + i] = gl
            gm = tiles(gl) * real(a0 + i)[None]
            sa = sa + jnp.sum(gm, axis=0)
            sb = sb + jnp.sum(gm * tiles(centred * rstd1), axis=0)
        return sa, sb

    with jax.named_scope("grad_act"):
        carry = blocks(gact_block, (zero16, zero16))
    all_start(3, jnp.concatenate([row_sum(carry[0]), row_sum(carry[1]), pad6], axis=0))
    with jax.named_scope("sum1"):
        all_next(3, add_up)

    def tap_body(tap, _):
        t = lax.dot_general(
            acth[pl.ds(tap, L)].reshape(z.total, C),
            gch[pl.ds(HALO, L)].reshape(z.total, C),
            first,
            preferred_element_type=f32,
        )
        gb[0, tap] = t[:, :H]
        gb[1, tap] = t[:, H:]
        return 0

    with jax.named_scope("tap_grad"):
        lax.fori_loop(0, TAPS, tap_body, 0)
    with jax.named_scope("sum1_wait"):
        sum1 = all_end(3, add_up)
    in_scale = gain1 * rstd1
    in_shift = in_scale * sum1[0:1] / count
    in_slope = in_scale * rstd1 * sum1[1:2] / count

    neighbour = (2 * chip + 1 - core, s)
    core_rows = pl.multiple_of(core * H, H)
    other_rows = pl.multiple_of((1 - core) * H, H)
    chip_rows = pl.multiple_of(c1 * slice_rows, slice_rows)
    spans = (pl.ds(0, TAPS), pl.ds(TAPS, 3))

    def grad_core(i):
        cut = (slice(None), spans[i])
        go(
            remote(
                gb.at[(*cut, pl.ds(other_rows, H))], gb_core.at[cut], sem_g.at[0, i, 0], sem_g.at[1, i, 0], neighbour
            )
        )

    def grad_chips(i):
        cut = (slice(None), spans[i])
        arrive(gb_core.at[cut], sem_g.at[1, i, 0])
        total = gb[(*cut, pl.ds(core_rows, H))] + gb_core[cut]
        if z.p1 == 1:
            gb_sum[cut] = total
            return
        gb_low[cut] = total.astype(bf)
        for d in range(1, z.p1):
            t = lax.rem(c1 + d, z.p1)
            go(
                remote(
                    gb_low.at[(*cut, pl.ds(pl.multiple_of(t * slice_rows, slice_rows), slice_rows))],
                    gb_chips.at[(c1, *cut)],
                    sem_g.at[0, i, d],
                    sem_g.at[1, i, d],
                    peer_b(t),
                )
            )

    def grad_pair(i):
        cut = (slice(None), spans[i])
        if z.p1 > 1:
            gb_chips[(c1, *cut)] = gb_low[(*cut, pl.ds(chip_rows, slice_rows))]
            for d in range(1, z.p1):
                arrive(gb_chips.at[(lax.rem(c1 + z.p1 - d, z.p1), *cut)], sem_g.at[1, i, d])
            gb_sum[cut] = add_up([gb_chips[(p, *cut)].astype(f32) for p in range(z.p1)])
        if z.p2 > 1:
            gb_far[(c2, *cut)] = gb_sum[cut]
            for d in range(1, z.p2):
                t = lax.rem(c2 + d, z.p2)
                go(
                    remote(
                        gb_far.at[(c2, *cut)],
                        gb_far.at[(c2, *cut)],
                        sem_g.at[0, i, 24 + d],
                        sem_g.at[1, i, 24 + d],
                        peer_c(t),
                    )
                )
            for d in range(1, z.p2):
                arrive(gb_far.at[(lax.rem(c2 + z.p2 - d, z.p2), *cut)], sem_g.at[1, i, 24 + d])
            gb_sum[cut] = add_up([gb_far[(p, *cut)] for p in range(z.p2)])
        go(remote(gb_sum.at[o, spans[i]], gb_pair.at[spans[i]], sem_g.at[0, i, 8], sem_g.at[1, i, 8], partner))

    def grad_back(i):
        arrive(gb_pair.at[spans[i]], sem_g.at[1, i, 8])
        mine = gb_sum[s, spans[i]]
        other = gb_pair[spans[i]]
        own = pl.multiple_of(core_rows + chip_rows, slice_rows)
        gb_all[spans[i], pl.ds(own, slice_rows)] = mine + other
        at = gb_all.at[spans[i], pl.ds(own, slice_rows)]
        for d in range(1, z.p1):
            t = lax.rem(c1 + d, z.p1)
            go(remote(at, at, sem_g.at[0, i, 8 + d], sem_g.at[1, i, 8 + d], peer_b(t)))

    def grad_last(i):
        for d in range(1, z.p1):
            t = lax.rem(c1 + z.p1 - d, z.p1)
            at = pl.multiple_of(core_rows + t * slice_rows, slice_rows)
            arrive(gb_all.at[spans[i], pl.ds(at, slice_rows)], sem_g.at[1, i, 8 + d])
        at = gb_all.at[spans[i], pl.ds(core_rows, H)]
        go(remote(at, at, sem_g.at[0, i, 16], sem_g.at[1, i, 16], neighbour))

    def grad_done(i):
        arrive(gb_all.at[spans[i], pl.ds(other_rows, H)], sem_g.at[1, i, 16])

    grad_core(0)

    def input_body(a, _):
        gs = back(conv[a], summed[a].reshape(R, C) - mean1, in_scale, in_shift, in_slope)
        gs = times(gs, real(a)).astype(bf)
        gch[a + HALO] = tiles(gs)
        parts[0] = gs.astype(f32).reshape(J, RW, C)
        link(lambda v: parts[0, v], 1)
        for w in range(J):
            at = slice(w * RW, (w + 1) * RW)
            mixed[0, at] = (parts[0, w] * edge[0, w : w + 1]).astype(bf)
            mixed[1, at] = chain[kin[1, w]].astype(bf)
            mixed[2, at] = (parts[0, par[w]] * edge[2, w : w + 1]).astype(bf)
        t = whole(ct, a).astype(f32)
        for k in range(3):
            t = t + lax.dot_general(mixed[k], ws[:, k * C : (k + 1) * C], last, preferred_element_type=f32)
        put(iz, a, t.astype(bf))
        return 0

    for j, (a0, a1) in enumerate(z.chunks):
        with jax.named_scope("input_grad"):
            lax.fori_loop(a0, a1, input_body, 0)
        ship(iz, ing_own, ing_rcv, sem_i, j)
        with jax.named_scope("grad_reduce"):
            if j == 0:
                grad_chips(0)
            if j == n_chunks - 1:
                grad_pair(0)

    def edge_rows_f(v):
        return jnp.concatenate(
            [xh[0, :, pl.ds(v, 1)].reshape(L * RW, H), xh[1, :, pl.ds(v, 1)].reshape(L * RW, H)], axis=1
        )

    def edge_rows_g(v):
        return gch[pl.ds(HALO, L), pl.ds(v, 1)].reshape(L * RW, C)

    sg[...] = jnp.zeros_like(sg)

    def edge_body(v, acc):
        pv = par[v]
        hot = jnp.where(lax.broadcasted_iota(jnp.int32, (8, C), 1) == v, 1.0, 0.0)
        kind = lax.broadcasted_iota(jnp.int32, (8, C), 0)
        far = jnp.where(v > 0, 1.0, 0.0)
        f_v, g_v = edge_rows_f(v), edge_rows_g(v)
        f_p, g_p = edge_rows_f(pv), edge_rows_g(pv)
        for k, (fx, gx, on) in enumerate(((f_v, g_v, 1.0), (f_p, g_v, far), (f_v, g_p, far))):
            prod = lax.dot_general(fx, gx, first, preferred_element_type=f32)
            sg[k] = sg[k] + prod * edge[k, pl.ds(v, 1)]
            dot = jnp.sum(row_sum(prod * ws[:, k * C : (k + 1) * C].astype(f32)), axis=1, keepdims=True)
            acc = acc + jnp.where(kind == k, hot, 0.0) * (dot * on)
        return acc

    with jax.named_scope("edges"):
        dvec = lax.fori_loop(0, J, edge_body, jnp.zeros((8, C), f32))
    for j in range(6):
        k, h = j // 2, j % 2
        gb[j // 3, TAPS + j % 3] = sg[k, :, h * H : (h + 1) * H]
    grad_core(1)
    all_start(4, dvec)
    with jax.named_scope("grad_reduce"):
        grad_back(0)
        grad_chips(1)
        all_next(4, add_up)
        grad_pair(1)
        grad_back(1)
        grad_last(0)
        dvec = all_end(4, add_up)
        grad_last(1)
    for k in range(3):
        per_edge = dvec[k : k + 1, :J]
        if k == 1:
            per_edge = lax.dot_general(
                eye, jnp.broadcast_to(per_edge, (J, J)), last, precision=exact_mode, preferred_element_type=f32
            )
        ig_out[k] = adj[k] * per_edge
    for i, row in enumerate((sum1[1:2], sum1[0:1], sum2[1:2], sum2[0:1])):
        sums_out[i : i + 1] = jnp.where(s == 0, row[:, :H], row[:, H:])
    sums_out[4:8] = jnp.zeros((4, H), f32)
    with jax.named_scope("grad_reduce_end"):
        grad_done(0)
        grad_done(1)
        last_out = [pltpu.make_async_copy(gb_all.at[pl.ds(0, TAPS)], tg_out, sem_l.at[2, 2])]
        for j in range(3):
            last_out.append(
                pltpu.make_async_copy(gb_all.at[TAPS + j], sg_out.at[:, pl.ds(j * H, H)], sem_l.at[2, 3 + j])
            )
        for cp in last_out:
            cp.start()

    with jax.named_scope("last_waits"):
        for j in range(n_chunks):
            a0, a1 = z.chunks[j]
            at = pl.ds(a0, a1 - a0)
            arrive(act_rcv.at[at], sem_a.at[1, j])
            arrive(ing_rcv.at[at], sem_i.at[1, j])
        for cp in outs + last_out:
            cp.wait()
        for cp in sends:
            cp.wait_send()


def finish(
    z,
    act_own,
    act_rcv,
    ing_own,
    ing_rcv,
    tg_in,
    sg_in,
    sums_in,
    ig_in,
    act_out,
    ing_out,
    tg_out,
    sg_out,
    r0,
    r1,
    r2,
    r3,
    ig_out,
    low,
    full,
    tg,
    sg,
    sem_in,
    sem_out,
):
    J, L = z.joints, z.blk
    s = lax.axis_index("sub")
    jobs = [(act_own, act_out, s), (ing_own, ing_out, s), (act_rcv, act_out, 1 - s), (ing_rcv, ing_out, 1 - s)]
    ins = []
    for i, (src, _, _) in enumerate(jobs):
        cp = pltpu.make_async_copy(src, low.at[i], sem_in.at[i])
        cp.start()
        ins.append(cp)
    grads = []
    for i, (src, mid, dst) in enumerate(((tg_in, tg, tg_out), (sg_in, sg, sg_out))):
        cp = pltpu.make_async_copy(src, mid, sem_in.at[4 + i])
        cp.start()
        grads.append((cp, pltpu.make_async_copy(mid, dst, sem_in.at[6 + i])))
    for i, r in enumerate((r0, r1, r2, r3)):
        r[...] = sums_in[i : i + 1]
    ig_out[...] = ig_in[...]
    cut = L - z.pad

    def pieces(i, dst, w):
        for part, (a0, a1) in enumerate(z.locals):
            for b in range(NB):
                cp = pltpu.make_async_copy(
                    full.at[i, pl.ds(a0, a1 - a0), :, b],
                    dst.at[pl.ds(w * z.win + b * L + a0, a1 - a0)],
                    sem_out.at[i, part, b],
                )
                yield part == 1 and b == NB - 1, cp

    for i, (_, dst, w) in enumerate(jobs):
        ins[i].wait()

        def body(a, _, i=i):
            value = low[i, a].reshape(z.rows, z.half).astype(jnp.float32)
            full[i, a] = value.reshape(J, NB, 2, z.half)
            return 0

        lax.fori_loop(0, L, body, 0)
        for beyond, cp in pieces(i, dst, w):
            if beyond:
                pl.when(w == 0)(cp.start)
            else:
                cp.start()
    for cp_in, cp_out in grads:
        cp_in.wait()
        cp_out.start()
    for _, cp_out in grads:
        cp_out.wait()
    for i, (_, dst, w) in enumerate(jobs):
        for beyond, cp in pieces(i, dst, w):
            if beyond:
                pl.when(w == 0)(cp.wait)
            else:
                cp.wait()


def block(
    n_dp, features, presence, parents, w_spatial, importance, gain_one, shift_one, w_temporal, gain_two, shift_two, cotangent
):
    _, _, frames, joints, half = features.shape
    z = Sizes(n_dp, frames, joints, half)
    f32, bf = jnp.float32, jnp.bfloat16
    C, H, L, R, J = z.chan, z.half, z.blk, z.rows, z.joints

    def natural(x):
        return x.transpose(0, 2, 3, 1, 4).reshape(frames, joints, 2, half)

    any_, vmem, smem = (pl.BlockSpec(memory_space=m) for m in (pl.ANY, pltpu.VMEM, pltpu.SMEM))
    blocked = (L, J, NB, 2, H)
    sds = jax.ShapeDtypeStruct
    VM, DMA = pltpu.VMEM, pltpu.SemaphoreType.DMA
    nch = len(z.chunks)
    outs = pl.pallas_call(
        functools.partial(mega, z),
        name="graph_conv_block",
        out_shape=[sds(blocked, bf)] * 4
        + [sds((TAPS, C, H), f32), sds((C, 3 * H), f32), sds((8, H), f32), sds((3, J, J), f32)],
        in_specs=[any_] * 4 + [vmem, smem, smem] + [vmem] * 4,
        out_specs=[any_] * 6 + [vmem] * 2,
        scratch_shapes=[
            VM((2,) + blocked, bf),
            VM((2,) + blocked, bf),
            VM((TAPS, C, C), bf),
            VM((C, 3 * C), bf),
            VM((3, J, RW, C), f32),
            VM((J, RW, C), f32),
            VM((3, R, C), bf),
            VM((L, J, RW, C), f32),
            VM((L + 2 * HALO, J, RW, C), bf),
            VM((L, R, C), f32),
            VM((L + 2 * HALO, J, RW, C), bf),
            VM((2,) + blocked, bf),
            VM((2,) + blocked, bf),
            VM((2, TAPS + 3, C, H), f32),
            VM((2, TAPS + 3, H, H), f32),
            VM((2, TAPS + 3, H, H), bf),
            VM((z.p1, 2, TAPS + 3, H // z.p1, H), bf),
            VM((z.p2, 2, TAPS + 3, H // z.p1, H), f32),
            VM((2, TAPS + 3, H // z.p1, H), f32),
            VM((TAPS + 3, H // z.p1, H), f32),
            VM((TAPS + 3, C, H), f32),
            VM((3, C, C), f32),
            VM((2, 8, H), f32),
            VM((3, J, J), f32),
            VM((3, J, C), f32),
            pltpu.SMEM((2, J), jnp.int32),
            VM((3, HALO, 64, C), bf),
            VM((3, HALO, 64, C), bf),
            VM((5, 4, 8, C), f32),
            VM((5, z.p1, 8, C), f32),
            VM((5, max(z.p2, 2), 8, C), f32),
            DMA((3, 2 * NB)),
            DMA((2, nch, NB)),
            DMA((2, nch, NB)),
            DMA((3, nch)),
            DMA((3, nch)),
            DMA((2, 40)),
            DMA((2, 4)),
            DMA((2, 2, 32)),
            DMA((2, 5, 4)),
            DMA((2, 5, z.p1)),
            DMA((2, 5, max(z.p2, 2))),
        ],
        compiler_params=pltpu.CompilerParams(
            collective_id=0, has_side_effects=True, vmem_limit_bytes=62 * 2**20
        ),
    )(
        natural(features),
        natural(cotangent),
        w_temporal,
        w_spatial,
        importance,
        parents,
        presence,
        *(v.reshape(1, H) for v in (gain_one, shift_one, gain_two, shift_two)),
    )
    act, ing, tg, sg, r0, r1, r2, r3, ig = pl.pallas_call(
        functools.partial(finish, z),
        name="natural_order",
        out_shape=[sds((frames, joints, 2, H), f32)] * 2
        + [sds((TAPS, C, H), f32), sds((C, 3 * H), f32)]
        + [sds((1, H), f32)] * 4
        + [sds((3, J, J), f32)],
        in_specs=[any_] * 6 + [vmem] * 2,
        out_specs=[any_] * 4 + [vmem] * 5,
        scratch_shapes=[
            VM((4,) + blocked, bf),
            VM((4,) + blocked, f32),
            VM((TAPS, C, H), f32),
            VM((C, 3 * H), f32),
            DMA((8,)),
            DMA((4, 2, NB)),
        ],
        compiler_params=pltpu.CompilerParams(vmem_limit_bytes=60 * 2**20),
    )(*outs)

    def back(x):
        return x.reshape(1, frames, joints, 2, half).transpose(0, 3, 1, 2, 4)

    return (
        back(act),
        back(ing),
        sg,
        ig,
        *(r.reshape(H) for r in (r0, r1)),
        tg,
        *(r.reshape(H) for r in (r2, r3)),
    )


def solution(mesh):
    in_specs = (
        P("dp", None, None, None, "sub"),
        P("dp", None),
        P(),
        P(None, "sub"),
        P(),
        P("sub"),
        P("sub"),
        P(None, None, "sub"),
        P("sub"),
        P("sub"),
        P("dp", None, None, None, "sub"),
    )
    out_specs = (
        P("dp", None, None, None, "sub"),
        P("dp", None, None, None, "sub"),
        P(None, "sub"),
        P(),
        P("sub"),
        P("sub"),
        P(None, None, "sub"),
        P("sub"),
        P("sub"),
    )
    return jax.shard_map(
        functools.partial(block, mesh.shape["dp"]), mesh=mesh, in_specs=in_specs, out_specs=out_specs, check_vma=False
    )
```

time: 1940 us -> 312 us (0.16)
  local copies, waits for them, and re-layouts: 626 us -> 0 us
  waiting for transfers between devices: 586 us -> 0 us
  matrix products: 387 us -> 0 us
  Pallas kernels: 0 us -> 311 us
  blocking collectives: 226 us -> 0 us
  other arithmetic: 84.9 us -> 0 us
    dot_general x37 -> x0, matrix products: 387 us -> none  [the longest x9 76.1 us: temporal_input_grad(): lax.dot_general(flatten_rows(window), weights[tap_index], column_contract...]
    reduce_scatter x2 -> x0, waiting for transfers between devices: 348 us -> none  [the longest x1 175 us: local(): summed = lax.psum_scatter(term, 'sub', scatter_dimension=4, tiled=True)]
    pallas_call x0 -> x2, Pallas kernels: none -> 311 us  [the longest x1 299 us: block(): pl.pallas_call(functools.partial(mega, z), name='graph_conv_block', out_s...]
    reshape x23 -> x0, local copies, waits for them, and re-layouts: 255 us -> none  [the longest x19 198 us: flatten_rows(): return values.reshape(-1, values.shape[-1])]
    all_gather x3 -> x0, waiting for transfers between devices: 227 us -> none  [the longest x1 97.9 us: local(): whole_inputs = lax.all_gather(features, 'sub', axis=4, tiled=True)]
    psum x7 -> x0, blocking collectives: 226 us -> none  [the longest x2 66.3 us: statistics(): lax.psum(jnp.sum(centered * centered * present_weight, axis=(0, 1, 2, 3))...]
    slice x18 -> x0, local copies, waits for them, and re-layouts: 187 us -> none  [the longest x9 135 us: temporal(): window = padded[:, :, tap_index:tap_index + frames]]
    unnamed x127 -> x0, local copies, waits for them, and re-layouts: 86.4 us -> none
  transfers between devices with their start and end apart: 7 -> 0, of which waited for: 6 -> 0; matrix products, arithmetic and copies ran while one was open for 10% -> 0% of each run, Pallas kernels for 0% -> 0%
where the time goes in v1:
time: 312 us
  Pallas kernels  311 us (100%)
    pallas_call x1, Pallas kernels, block(): pl.pallas_call(functools.partial(mega, z), name='graph_conv_block', out_s...  299 us
    pallas_call x1, Pallas kernels, block(): pl.pallas_call(functools.partial(finish, z), name='natural_order', out_sh...  11.7 us

profile of v1, /device:TPU:1, one launch (start us, length us, event | category | flops | bytes accessed | tf_op | source)
XLA Modules:
  0.0 311.5 jit_solution(11645696524467724412)
XLA Ops:
  0.6 299.0 %graph_conv_block.1 = (bf16[19,25,8,2,128]{4,3,2,1,0:T(2,128)(2,1)}, bf16[19,25,8,2,128]{4,3,2,1,0:T(2,128)(2,1)}, bf16[19,25,8,2,128]{4,3,2,1,0:T(2,128)(2,1)},...) custom-call(bf16[300,25,2,128]{3,2,1,0:T(2,128)(2,1)} %bitcast.20, ...), custom_call_target="tpu_custom_call" | custom-call | tf_op jit(solution)/shard_map/graph_conv_block/pallas_call | solution.py:886
  299.7 11.7 %natural_order.1 = (f32[300,25,2,128]{3,2,1,0:T(2,128)}, f32[300,25,2,128]{3,2,1,0:T(2,128)}, f32[9,256,128]{2,1,0:T(8,128)}, f32[256,384]{1,0:T(8,128)}, f32[1,...) custom-call(bf16[19,25,8,2,128]{4,3,2,1,0:T(2,128)(2,1)} %get-tuple-element.26, ...), custom_call_target="tpu_custom_call" | custom-call | tf_op jit(solution)/shard_map/natural_order/pallas_call | solution.py:950

commit v2 on v1

--- a/solution.py
+++ b/solution.py
@@ -42,8 +42,11 @@
         self.rows = joints * RW
         self.total = self.blk * self.rows
         self.chips = n_dp // 2
-        self.p1 = min(8, self.chips)
+        self.p1 = 8
         self.p2 = self.chips // self.p1
+        self.quads = n_dp // 4
+        self.q1 = 4
+        self.q2 = self.quads // self.q1
         cut = self.blk - self.pad
         step = -(-cut // 3)
         self.chunks = [(a, min(a + step, cut)) for a in range(0, cut, step)]
@@ -100,10 +103,12 @@
     edge,
     kin,
     halo_s,
+    halo_m,
     halo_r,
     arA,
     arB,
     arC,
+    arD,
     sem_l,
     sem_f,
     sem_c,
@@ -115,6 +120,7 @@
     semA,
     semB,
     semC,
+    semD,
 ):
     f32, bf = jnp.float32, jnp.bfloat16
     J, C, H, L, R = z.joints, z.chan, z.half, z.blk, z.rows
@@ -127,14 +133,34 @@
     c2 = lax.div(chip, z.p1)
     partner = (dp, o)
 
-    def peer_a(t):
-        return (2 * chip + lax.div(t, 2), lax.rem(t, 2))
+    quad = lax.div(dp, 4)
+    q0 = lax.rem(dp, 4)
+    q1 = lax.rem(quad, z.q1)
+    q2 = lax.div(quad, z.q1)
+    flip = dp + 4 - 8 * lax.rem(quad, 2)
+    across = (flip, o)
+    beside = (flip, s)
 
     def peer_b(t):
         return (2 * (c2 * z.p1 + t) + core, s)
 
     def peer_c(t):
         return (2 * (t * z.p1 + c1) + core, s)
+
+    def peer_0(t):
+        return (4 * quad + t, s)
+
+    def peer_1(t):
+        return (4 * (q2 * z.q1 + t) + q0, s)
+
+    def peer_2(t):
+        return (4 * (t * z.q1 + q1) + q0, s)
+
+    def other_chip(t):
+        return t + 2 - 4 * lax.rem(lax.div(t, 2), 2)
+
+    def owned(t):
+        return t + s * (other_chip(t) - t)
 
     def remote(src, dst, ssem, rsem, dev):
         return pltpu.make_async_remote_copy(
@@ -173,17 +199,13 @@
         prm[s, i : i + 1] = v[...]
 
     bar = pltpu.get_barrier_semaphore()
-    qa = core * 2 + s
-    n_peers = 0
-    for d in range(1, 4):
-        pl.semaphore_signal(bar, inc=1, device_id=peer_a(lax.rem(qa + d, 4)), device_id_type=MESH)
-        n_peers += 1
-    for d in range(1, z.p1):
-        pl.semaphore_signal(bar, inc=1, device_id=peer_b(lax.rem(c1 + d, z.p1)), device_id_type=MESH)
-        n_peers += 1
-    for d in range(1, z.p2):
-        pl.semaphore_signal(bar, inc=1, device_id=peer_c(lax.rem(c2 + d, z.p2)), device_id_type=MESH)
-        n_peers += 1
+    greeted = [partner, across, (2 * chip + 1 - core, s)]
+    greeted += [peer_b(lax.rem(c1 + d, z.p1)) for d in range(1, z.p1)]
+    greeted += [peer_c(lax.rem(c2 + d, z.p2)) for d in range(1, z.p2)]
+    greeted += [(4 * quad + 3 - q0, s)]
+    n_peers = len(greeted)
+    for dev in greeted:
+        pl.semaphore_signal(bar, inc=1, device_id=dev, device_id_type=MESH)
     with jax.named_scope("barrier"):
         pl.semaphore_wait(bar, n_peers)
 
@@ -231,6 +253,8 @@
     n_chunks = len(z.chunks)
     for j in range(n_chunks):
         send_rows(feat, xh, sem_f, j)
+    for j in range(n_chunks):
+        send_rows(cot, ct, sem_c, j)
 
     ri = lax.broadcasted_iota(jnp.int32, (J, J), 0)
     ci = lax.broadcasted_iota(jnp.int32, (J, J), 1)
@@ -352,21 +376,22 @@
         return jnp.concatenate([n, mean, spread_up, jnp.zeros((5, C), f32)], axis=0)
 
     def all_start(r, val):
-        spread(arA, semA, r, qa, 4, peer_a, val)
+        spread(arA, semA, r, q0, 4, peer_0, val)
 
     def all_next(r, join):
-        val = join(gather(arA, semA, r, qa, 4))
-        if z.p1 > 1:
-            spread(arB, semB, r, c1, z.p1, peer_b, val)
-        else:
-            arB[r, 0] = val
+        spread(arB, semB, r, q1, z.q1, peer_1, join(gather(arA, semA, r, q0, 4)))
+
+    def all_more(r, join):
+        val = join(gather(arB, semB, r, q1, z.q1))
+        if z.q2 > 1:
+            spread(arC, semC, r, q2, z.q2, peer_2, val)
+            val = join(gather(arC, semC, r, q2, z.q2))
+        arD[r, s] = val
+        go(remote(arD.at[r, s], arD.at[r, s], semD.at[0, r], semD.at[1, r], across))
 
     def all_end(r, join):
-        val = join(gather(arB, semB, r, c1, z.p1))
-        if z.p2 > 1:
-            spread(arC, semC, r, c2, z.p2, peer_c, val)
-            val = join(gather(arC, semC, r, c2, z.p2))
-        return val
+        arrive(arD.at[r, o], semD.at[1, r])
+        return join([arD[r, 0], arD[r, 1]])
 
     def moments(val_k, s1, s2):
         n = (p0 + p1) * (z.win - z.pad * side) * J
@@ -408,9 +433,6 @@
     for j, (a0, a1) in enumerate(z.chunks):
         with jax.named_scope("features_wait"):
             take_rows(xh, sem_f, j)
-        if j == n_chunks - 1:
-            for i in range(n_chunks):
-                send_rows(cot, ct, sem_c, i)
         with jax.named_scope("spatial"):
             carry = lax.fori_loop(a0, a1, spatial_body, carry)
 
@@ -422,13 +444,21 @@
     ).astype(bf)
     edge_a = (L - HALO) * o
 
-    def halo_out(ref, slot, i):
-        for h in range(HALO):
-            halo_s[slot, h] = jnp.dot(pick, ref(edge_a + h).astype(bf), preferred_element_type=f32).astype(bf)
-        go(remote(halo_s.at[slot], halo_r.at[slot], sem_h.at[0, i], sem_h.at[1, i], partner))
-
-    def halo_in(slot, i):
-        arrive(halo_r.at[slot], sem_h.at[1, i])
+    def halo_out(r, refs):
+        for i, ref in enumerate(refs):
+            for h in range(HALO):
+                row = jnp.dot(pick, ref(edge_a + h).astype(bf), preferred_element_type=f32)
+                halo_s[r + i, h] = row.astype(bf)
+        at = pl.ds(r, len(refs))
+        go(remote(halo_s.at[at], halo_m.at[at], sem_h.at[0, r, 0], sem_h.at[1, r, 0], across))
+
+    def halo_relay(r, n):
+        at = pl.ds(r, n)
+        arrive(halo_m.at[at], sem_h.at[1, r, 0])
+        go(remote(halo_m.at[at], halo_r.at[at], sem_h.at[0, r, 1], sem_h.at[1, r, 1], beside))
+
+    def halo_in(r, n):
+        arrive(halo_r.at[pl.ds(r, n)], sem_h.at[1, r, 1])
 
     row_in = lax.broadcasted_iota(jnp.int32, (R, C), 0) & (RW - 1)
     fside = 1.0 - side
@@ -443,10 +473,12 @@
             upper = jnp.where(row_in >= RW - 2, extra * fside, upper)
             buf[HALO + L + h] = tiles(upper.astype(bf))
 
-    halo_out(lambda a: summed[a].reshape(R, C), 0, 0)
+    halo_out(0, [lambda a: summed[a].reshape(R, C)])
     all_start(0, moments(*carry))
     with jax.named_scope("st1"):
         all_next(0, merge)
+        halo_relay(0, 1)
+        all_more(0, merge)
         st1 = all_end(0, merge)
     count = jnp.maximum(st1[0:1], 1.0)
     mean1 = st1[1:2]
@@ -461,7 +493,7 @@
 
     with jax.named_scope("act"):
         lax.fori_loop(0, L, act_body, 0)
-    halo_in(0, 0)
+    halo_in(0, 1)
     fill_halo(acth, lambda h: gelu((halo_r[0, h].astype(f32) - mean1) * scale1 + shift1).astype(bf))
 
     arrive(wt_at(o, theirs, H), sem_w.at[1, 37])
@@ -492,6 +524,7 @@
     all_start(1, moments(*carry))
     with jax.named_scope("st2"):
         all_next(1, merge)
+        all_more(1, merge)
         st2 = all_end(1, merge)
     mean2 = st2[1:2]
     rstd2 = lax.rsqrt(st2[2:3] / count + norm_eps)
@@ -530,12 +563,13 @@
             carry = lax.fori_loop(a0, a1, out_body, carry)
         ship(zz, act_own, act_rcv, sem_a, j)
 
-    halo_out(lambda a: conv[a], 1, 1)
-    halo_out(lambda a: whole(ct, a), 2, 2)
+    halo_out(1, [lambda a: conv[a], lambda a: whole(ct, a)])
     pad6 = jnp.zeros((6, C), f32)
     all_start(2, jnp.concatenate([row_sum(carry[0]), row_sum(carry[1]), pad6], axis=0))
     with jax.named_scope("sum2"):
         all_next(2, add_up)
+        halo_relay(1, 2)
+        all_more(2, add_up)
         sum2 = all_end(2, add_up)
     out_scale = gain2 * rstd2
     out_shift = out_scale * sum2[0:1] / count
@@ -554,8 +588,7 @@
 
     with jax.named_scope("gconv"):
         lax.fori_loop(0, L, gconv_body, 0)
-    halo_in(1, 1)
-    halo_in(2, 2)
+    halo_in(1, 2)
     fill_halo(
         gch,
         lambda h: back(halo_r[1, h].astype(f32), halo_r[2, h].astype(f32), out_scale, out_shift, out_slope).astype(bf),
@@ -596,7 +629,9 @@
         return 0
 
     with jax.named_scope("tap_grad"):
-        lax.fori_loop(0, TAPS, tap_body, 0)
+        lax.fori_loop(0, TAPS // 2, tap_body, 0)
+        all_more(3, add_up)
+        lax.fori_loop(TAPS // 2, TAPS, tap_body, 0)
     with jax.named_scope("sum1_wait"):
         sum1 = all_end(3, add_up)
     in_scale = gain1 * rstd1
@@ -606,7 +641,10 @@
     neighbour = (2 * chip + 1 - core, s)
     core_rows = pl.multiple_of(core * H, H)
     other_rows = pl.multiple_of((1 - core) * H, H)
-    chip_rows = pl.multiple_of(c1 * slice_rows, slice_rows)
+    def slice_of(t):
+        return pl.multiple_of(owned(t) * slice_rows, slice_rows)
+
+    chip_rows = slice_of(c1)
     spans = (pl.ds(0, TAPS), pl.ds(TAPS, 3))
 
     def grad_core(i):
@@ -621,15 +659,12 @@
         cut = (slice(None), spans[i])
         arrive(gb_core.at[cut], sem_g.at[1, i, 0])
         total = gb[(*cut, pl.ds(core_rows, H))] + gb_core[cut]
-        if z.p1 == 1:
-            gb_sum[cut] = total
-            return
         gb_low[cut] = total.astype(bf)
         for d in range(1, z.p1):
             t = lax.rem(c1 + d, z.p1)
             go(
                 remote(
-                    gb_low.at[(*cut, pl.ds(pl.multiple_of(t * slice_rows, slice_rows), slice_rows))],
+                    gb_low.at[(*cut, pl.ds(slice_of(t), slice_rows))],
                     gb_chips.at[(c1, *cut)],
                     sem_g.at[0, i, d],
                     sem_g.at[1, i, d],
@@ -639,11 +674,10 @@
 
     def grad_pair(i):
         cut = (slice(None), spans[i])
-        if z.p1 > 1:
-            gb_chips[(c1, *cut)] = gb_low[(*cut, pl.ds(chip_rows, slice_rows))]
-            for d in range(1, z.p1):
-                arrive(gb_chips.at[(lax.rem(c1 + z.p1 - d, z.p1), *cut)], sem_g.at[1, i, d])
-            gb_sum[cut] = add_up([gb_chips[(p, *cut)].astype(f32) for p in range(z.p1)])
+        gb_chips[(c1, *cut)] = gb_low[(*cut, pl.ds(chip_rows, slice_rows))]
+        for d in range(1, z.p1):
+            arrive(gb_chips.at[(lax.rem(c1 + z.p1 - d, z.p1), *cut)], sem_g.at[1, i, d])
+        gb_sum[cut] = add_up([gb_chips[(p, *cut)].astype(f32) for p in range(z.p1)])
         if z.p2 > 1:
             gb_far[(c2, *cut)] = gb_sum[cut]
             for d in range(1, z.p2):
@@ -660,7 +694,7 @@
             for d in range(1, z.p2):
                 arrive(gb_far.at[(lax.rem(c2 + z.p2 - d, z.p2), *cut)], sem_g.at[1, i, 24 + d])
             gb_sum[cut] = add_up([gb_far[(p, *cut)] for p in range(z.p2)])
-        go(remote(gb_sum.at[o, spans[i]], gb_pair.at[spans[i]], sem_g.at[0, i, 8], sem_g.at[1, i, 8], partner))
+        go(remote(gb_sum.at[o, spans[i]], gb_pair.at[spans[i]], sem_g.at[0, i, 8], sem_g.at[1, i, 8], across))
 
     def grad_back(i):
         arrive(gb_pair.at[spans[i]], sem_g.at[1, i, 8])
@@ -676,7 +710,7 @@
     def grad_last(i):
         for d in range(1, z.p1):
             t = lax.rem(c1 + z.p1 - d, z.p1)
-            at = pl.multiple_of(core_rows + t * slice_rows, slice_rows)
+            at = pl.multiple_of(core_rows + slice_of(t), slice_rows)
             arrive(gb_all.at[spans[i], pl.ds(at, slice_rows)], sem_g.at[1, i, 8 + d])
         at = gb_all.at[spans[i], pl.ds(core_rows, H)]
         go(remote(at, at, sem_g.at[0, i, 16], sem_g.at[1, i, 16], neighbour))
@@ -748,6 +782,7 @@
         grad_back(0)
         grad_chips(1)
         all_next(4, add_up)
+        all_more(4, add_up)
         grad_pair(1)
         grad_back(1)
         grad_last(0)
@@ -919,20 +954,23 @@
             pltpu.SMEM((2, J), jnp.int32),
             VM((3, HALO, 64, C), bf),
             VM((3, HALO, 64, C), bf),
+            VM((3, HALO, 64, C), bf),
             VM((5, 4, 8, C), f32),
-            VM((5, z.p1, 8, C), f32),
-            VM((5, max(z.p2, 2), 8, C), f32),
+            VM((5, z.q1, 8, C), f32),
+            VM((5, z.q2, 8, C), f32),
+            VM((5, 2, 8, C), f32),
             DMA((3, 2 * NB)),
             DMA((2, nch, NB)),
             DMA((2, nch, NB)),
             DMA((3, nch)),
             DMA((3, nch)),
             DMA((2, 40)),
-            DMA((2, 4)),
+            DMA((2, 2, 2)),
             DMA((2, 2, 32)),
             DMA((2, 5, 4)),
-            DMA((2, 5, z.p1)),
-            DMA((2, 5, max(z.p2, 2))),
+            DMA((2, 5, z.q1)),
+            DMA((2, 5, z.q2)),
+            DMA((2, 5)),
         ],
         compiler_params=pltpu.CompilerParams(
             collective_id=0, has_side_effects=True, vmem_limit_bytes=62 * 2**20

time: 312 us -> 234 us (0.75)
  Pallas kernels: 311 us -> 233 us
    pallas_call x1, Pallas kernels: 299 us -> 221 us  [block(): pl.pallas_call(functools.partial(mega, z), name='graph_conv_block', out_s...]
where the time goes in v2:
time: 234 us
  Pallas kernels  233 us (100%)
    pallas_call x1, Pallas kernels, block(): pl.pallas_call(functools.partial(mega, z), name='graph_conv_block', out_s...  221 us
    pallas_call x1, Pallas kernels, block(): pl.pallas_call(functools.partial(finish, z), name='natural_order', out_sh...  11.7 us

profile of v2, /device:TPU:1, one launch (start us, length us, event | category | flops | bytes accessed | tf_op | source)
XLA Modules:
  0.0 233.9 jit_solution(8297672565468201561)
XLA Ops:
  0.6 221.4 %graph_conv_block.1 = (bf16[19,25,8,2,128]{4,3,2,1,0:T(2,128)(2,1)}, bf16[19,25,8,2,128]{4,3,2,1,0:T(2,128)(2,1)}, bf16[19,25,8,2,128]{4,3,2,1,0:T(2,128)(2,1)},...) custom-call(bf16[300,25,2,128]{3,2,1,0:T(2,128)(2,1)} %bitcast.20, ...), custom_call_target="tpu_custom_call" | custom-call | tf_op jit(solution)/shard_map/graph_conv_block/pallas_call | solution.py:921
  222.0 11.7 %natural_order.1 = (f32[300,25,2,128]{3,2,1,0:T(2,128)}, f32[300,25,2,128]{3,2,1,0:T(2,128)}, f32[9,256,128]{2,1,0:T(8,128)}, f32[256,384]{1,0:T(8,128)}, f32[1,...) custom-call(bf16[19,25,8,2,128]{4,3,2,1,0:T(2,128)(2,1)} %get-tuple-element.26, ...), custom_call_target="tpu_custom_call" | custom-call | tf_op jit(solution)/shard_map/natural_order/pallas_call | solution.py:988

commit v3 on v2

--- a/solution.py
+++ b/solution.py
@@ -11,6 +11,7 @@
 exact_mode = lax.Precision.HIGHEST
 MESH = pl.DeviceIdType.MESH
 TAPS = 9
+EARLY = 7
 HALO = TAPS // 2
 NB = 8
 RW = 2 * NB
@@ -20,16 +21,15 @@
 
 
 def gelu(x):
-    t = jnp.tanh(tanh_scale * (x + tanh_cubic * x * x * x))
-    return 0.5 * x * (1.0 + t)
+    t = jnp.tanh(x * (tanh_scale + (tanh_scale * tanh_cubic) * (x * x)))
+    return x * (0.5 + 0.5 * t)
 
 
 def gelu_both(x):
     x2 = x * x
-    t = jnp.tanh(tanh_scale * x * (1.0 + tanh_cubic * x2))
-    h = 0.5 * (1.0 + t)
-    slope = h + 0.5 * x * (1.0 - t * t) * (tanh_scale + (3.0 * tanh_scale * tanh_cubic) * x2)
-    return x * h, slope
+    h = 0.5 + 0.5 * jnp.tanh(x * (tanh_scale + (tanh_scale * tanh_cubic) * x2))
+    rise = x * (2.0 * tanh_scale + (6.0 * tanh_scale * tanh_cubic) * x2)
+    return x * h, h + h * ((1.0 - h) * rise)
 
 
 class Sizes:
@@ -44,9 +44,7 @@
         self.chips = n_dp // 2
         self.p1 = 8
         self.p2 = self.chips // self.p1
-        self.quads = n_dp // 4
-        self.q1 = 4
-        self.q2 = self.quads // self.q1
+        self.near = 2 * self.p1
         cut = self.blk - self.pad
         step = -(-cut // 3)
         self.chunks = [(a, min(a + step, cut)) for a in range(0, cut, step)]
@@ -78,16 +76,13 @@
     ig_out,
     xh,
     ct,
+    fx,
     wt,
     ws,
-    parts,
-    chain,
-    mixed,
     summed,
     acth,
     conv,
     gch,
-    zz,
     iz,
     gb,
     gb_core,
@@ -96,8 +91,8 @@
     gb_far,
     gb_sum,
     gb_pair,
-    gb_all,
-    sg,
+    mixed,
+    dots,
     prm,
     adj,
     edge,
@@ -106,7 +101,6 @@
     halo_m,
     halo_r,
     arA,
-    arB,
     arC,
     arD,
     sem_l,
@@ -118,7 +112,6 @@
     sem_h,
     sem_g,
     semA,
-    semB,
     semC,
     semD,
 ):
@@ -133,11 +126,8 @@
     c2 = lax.div(chip, z.p1)
     partner = (dp, o)
 
-    quad = lax.div(dp, 4)
-    q0 = lax.rem(dp, 4)
-    q1 = lax.rem(quad, z.q1)
-    q2 = lax.div(quad, z.q1)
-    flip = dp + 4 - 8 * lax.rem(quad, 2)
+    d1 = lax.rem(dp, z.near)
+    flip = dp + 4 - 8 * lax.rem(lax.div(dp, 4), 2)
     across = (flip, o)
     beside = (flip, s)
 
@@ -148,13 +138,7 @@
         return (2 * (t * z.p1 + c1) + core, s)
 
     def peer_0(t):
-        return (4 * quad + t, s)
-
-    def peer_1(t):
-        return (4 * (q2 * z.q1 + t) + q0, s)
-
-    def peer_2(t):
-        return (4 * (t * z.q1 + q1) + q0, s)
+        return (c2 * z.near + t, s)
 
     def other_chip(t):
         return t + 2 - 4 * lax.rem(lax.div(t, 2), 2)
@@ -171,6 +155,13 @@
             device_id=dev,
             device_id_type=MESH,
         )
+
+    bar = pltpu.get_barrier_semaphore()
+    greeted = [partner, across]
+    greeted += [peer_0(lax.rem(d1 + d, z.near)) for d in range(1, z.near)]
+    greeted += [peer_c(lax.rem(c2 + d, z.p2)) for d in range(1, z.p2)]
+    for dev in greeted:
+        pl.semaphore_signal(bar, inc=1, device_id=dev, device_id_type=MESH)
 
     def frame_row(w, b, a0, a1):
         at = w * z.win + (b * L + a0)
@@ -198,16 +189,8 @@
     for i, v in enumerate((g1, b1, g2, b2)):
         prm[s, i : i + 1] = v[...]
 
-    bar = pltpu.get_barrier_semaphore()
-    greeted = [partner, across, (2 * chip + 1 - core, s)]
-    greeted += [peer_b(lax.rem(c1 + d, z.p1)) for d in range(1, z.p1)]
-    greeted += [peer_c(lax.rem(c2 + d, z.p2)) for d in range(1, z.p2)]
-    greeted += [(4 * quad + 3 - q0, s)]
-    n_peers = len(greeted)
-    for dev in greeted:
-        pl.semaphore_signal(bar, inc=1, device_id=dev, device_id_type=MESH)
     with jax.named_scope("barrier"):
-        pl.semaphore_wait(bar, n_peers)
+        pl.semaphore_wait(bar, len(greeted))
 
     slice_rows = H // z.p1
     row0 = pl.multiple_of(core * H + c1 * slice_rows, slice_rows)
@@ -290,7 +273,6 @@
         return 0
 
     lax.fori_loop(0, J, kin_body, 0)
-    chain[0] = jnp.zeros((RW, C), f32)
 
     for i, at in ((0, ws_at), (1, wt_at)):
         arrive(at(o, row0, slice_rows), sem_w.at[1, 1 + i])
@@ -326,19 +308,25 @@
     tail = jnp.where(ri16 >= RW - 2, 1.0, 0.0).astype(f32)
     side = s.astype(f32)
 
-    def real(a):
-        late = jnp.where(a >= L - z.pad, side, 0.0) if z.pad else 0.0
-        return 1.0 - tail * late
+    real = 1.0 - tail * side
+    cut = L - z.pad
 
     def tiles(x):
         return x.reshape(-1, RW, C)
 
-    def times(x, m):
-        return (tiles(x) * m[None]).reshape(x.shape)
+    def flat(x):
+        return x.reshape(R, C)
+
+    def keep(x, late):
+        return (tiles(x) * real[None]).reshape(x.shape) if late else x
 
     def down_rows(x):
         return jnp.sum(tiles(x), axis=0)
 
+    def each(body, carry):
+        carry = lax.fori_loop(0, cut, body(False), carry)
+        return lax.fori_loop(cut, L, body(True), carry) if z.pad else carry
+
     def row_sum(x):
         return jnp.sum(x, axis=0, keepdims=True)
 
@@ -349,6 +337,10 @@
         return jnp.concatenate([ref[0, a].reshape(R, H), ref[1, a].reshape(R, H)], axis=1)
 
     def put(ref, a, value):
+        for h in range(2):
+            ref[h, a] = value[:, h * H : (h + 1) * H].reshape(J, RW, H)
+
+    def land(ref, a, value):
         for h in range(2):
             ref[h, a] = value[:, h * H : (h + 1) * H].reshape(J, NB, 2, H)
 
@@ -376,16 +368,13 @@
         return jnp.concatenate([n, mean, spread_up, jnp.zeros((5, C), f32)], axis=0)
 
     def all_start(r, val):
-        spread(arA, semA, r, q0, 4, peer_0, val)
-
-    def all_next(r, join):
-        spread(arB, semB, r, q1, z.q1, peer_1, join(gather(arA, semA, r, q0, 4)))
+        spread(arA, semA, r, d1, z.near, peer_0, val)
 
     def all_more(r, join):
-        val = join(gather(arB, semB, r, q1, z.q1))
-        if z.q2 > 1:
-            spread(arC, semC, r, q2, z.q2, peer_2, val)
-            val = join(gather(arC, semC, r, q2, z.q2))
+        val = join(gather(arA, semA, r, d1, z.near))
+        if z.p2 > 1:
+            spread(arC, semC, r, c2, z.p2, peer_c, val)
+            val = join(gather(arC, semC, r, c2, z.p2))
         arD[r, s] = val
         go(remote(arD.at[r, s], arD.at[r, s], semD.at[0, r], semD.at[1, r], across))
 
@@ -401,30 +390,41 @@
             [jnp.zeros((1, C), f32) + n, val_k + s1 / below, s2 - s1 * s1 / below, jnp.zeros((5, C), f32)], axis=0
         )
 
+    def scaled(sums, rstd):
+        return jnp.concatenate([sums[0:1], sums[1:2] * rstd], axis=0)
+
     zero16 = jnp.zeros((RW, C), f32)
     zero1 = jnp.zeros((1, C), f32)
 
-    def link(value, k):
+    def spatial_chunk(a0, a1, carry):
+        k_shift, s1, s2 = carry
+        n = a1 - a0
+        span, up_at, down_at, link = pl.ds(a0, n), pl.ds(0, n), pl.ds(n, n), pl.ds(2 * n, n)
+
+        def body(i, _):
+            f = whole(xh, a0 + i)
+            put(fx, a0 + i, f)
+            for k, (buf, at) in enumerate(((summed, a0 + i), (conv, i), (conv, n + i))):
+                buf[at] = tiles(jnp.dot(f, ws[:, k * C : (k + 1) * C], preferred_element_type=f32))
+            return 0
+
+        lax.fori_loop(0, n, body, 0)
+        conv[link, 0] = jnp.zeros((n, RW, C), f32)
         for v in range(J - 1, 0, -1):
-            chain[v] = value(v) * edge[k, v : v + 1] + chain[kin[0, v]]
-
-    def spatial_body(a, carry):
-        k_shift, s1, s2 = carry
-        f = whole(xh, a)
-        for k in range(3):
-            parts[k] = jnp.dot(f, ws[:, k * C : (k + 1) * C], preferred_element_type=f32).reshape(J, RW, C)
-        link(lambda v: parts[2, v], 2)
+            conv[link, v] = conv[down_at, v] * edge[2, v : v + 1] + conv[link, kin[0, v]]
+        w = (pw * real if a0 >= cut else pw)[None]
         for v in range(J):
-            t = parts[0, v] * edge[0, v : v + 1] + chain[kin[1, v]]
+            t = summed[span, v] * edge[0, v : v + 1] + conv[link, kin[1, v]]
             if v:
-                t = t + parts[1, par[v]] * edge[1, v : v + 1]
-            summed[a, v] = t
-        t = summed[a].reshape(R, C)
-        k_shift = jnp.where(a == 0, row_sum(t) * (1.0 / R), k_shift)
-        w = pw * real(a)
-        d = tiles(t - k_shift)
-        wd = d * w[None]
-        return k_shift, s1 + jnp.sum(wd, axis=0), s2 + jnp.sum(wd * d, axis=0)
+                t = t + conv[up_at, par[v]] * edge[1, v : v + 1]
+            summed[span, v] = t
+            if a0 == 0 and v == 0:
+                k_shift = row_sum(jnp.sum(t, axis=0)) * (1.0 / (n * RW))
+            d = t - k_shift
+            wd = d * w
+            s1 = s1 + jnp.sum(wd, axis=0)
+            s2 = s2 + jnp.sum(wd * d, axis=0)
+        return k_shift, s1, s2
 
     carry = (zero1, zero16, zero16)
     n_local = len(z.locals) * NB
@@ -434,7 +434,7 @@
         with jax.named_scope("features_wait"):
             take_rows(xh, sem_f, j)
         with jax.named_scope("spatial"):
-            carry = lax.fori_loop(a0, a1, spatial_body, carry)
+            carry = spatial_chunk(a0, a1, carry)
 
     lane = lax.broadcasted_iota(jnp.int32, (64, R), 1)
     line = lax.broadcasted_iota(jnp.int32, (64, R), 0)
@@ -473,12 +473,11 @@
             upper = jnp.where(row_in >= RW - 2, extra * fside, upper)
             buf[HALO + L + h] = tiles(upper.astype(bf))
 
-    halo_out(0, [lambda a: summed[a].reshape(R, C)])
     all_start(0, moments(*carry))
+    halo_out(0, [lambda a: flat(summed[a])])
     with jax.named_scope("st1"):
-        all_next(0, merge)
+        all_more(0, merge)
         halo_relay(0, 1)
-        all_more(0, merge)
         st1 = all_end(0, merge)
     count = jnp.maximum(st1[0:1], 1.0)
     mean1 = st1[1:2]
@@ -486,27 +485,31 @@
     gain1, shift1 = param(0), param(1)
     scale1 = rstd1 * gain1
 
-    def act_body(a, _):
-        t = gelu((summed[a].reshape(R, C) - mean1) * scale1 + shift1)
-        acth[a + HALO] = tiles(times(t, real(a)).astype(bf))
-        return 0
+    def act_body(late):
+        def body(a, _):
+            t = gelu((flat(summed[a]) - mean1) * scale1 + shift1)
+            acth[a + HALO] = tiles(keep(t, late).astype(bf))
+            return 0
+
+        return body
 
     with jax.named_scope("act"):
-        lax.fori_loop(0, L, act_body, 0)
+        each(act_body, 0)
     halo_in(0, 1)
     fill_halo(acth, lambda h: gelu((halo_r[0, h].astype(f32) - mean1) * scale1 + shift1).astype(bf))
 
     arrive(wt_at(o, theirs, H), sem_w.at[1, 37])
 
-    def conv_block(a0, n, carry):
+    def conv_block(a0, late, carry):
         k_shift, s1, s2 = carry
+        n = len(late)
         t = jnp.zeros((n * R, C), f32)
         for tap in range(TAPS):
             t = t + jnp.dot(acth[pl.ds(a0 + tap, n)].reshape(n * R, C), wt[tap], preferred_element_type=f32)
-        conv[pl.ds(a0, n)] = t.reshape(n, R, C)
+        conv[pl.ds(a0, n)] = t.reshape(n, J, RW, C)
         k_shift = jnp.where(a0 == 0, row_sum(t[:R]) * (1.0 / R), k_shift)
         for i in range(n):
-            w = pw * real(a0 + i)
+            w = pw * real if late[i] else pw
             d = tiles(t[i * R : (i + 1) * R] - k_shift)
             wd = d * w[None]
             s1 = s1 + jnp.sum(wd, axis=0)
@@ -514,16 +517,16 @@
         return k_shift, s1, s2
 
     def blocks(fun, carry):
-        carry = lax.fori_loop(0, L // G, lambda i, c: fun(i * G, G, c), carry)
-        if L % G:
-            carry = fun(L // G * G, L % G, carry)
+        plain = cut // G
+        carry = lax.fori_loop(0, plain, lambda i, c: fun(i * G, [False] * G, c), carry)
+        for a0 in range(plain * G, L, G):
+            carry = fun(a0, [a >= cut for a in range(a0, min(a0 + G, L))], carry)
         return carry
 
     with jax.named_scope("conv"):
         carry = blocks(conv_block, (zero1, zero16, zero16))
     all_start(1, moments(*carry))
     with jax.named_scope("st2"):
-        all_next(1, merge)
         all_more(1, merge)
         st2 = all_end(1, merge)
     mean2 = st2[1:2]
@@ -533,17 +536,22 @@
     for cp in local[n_local:]:
         cp.wait()
 
-    def out_body(a, carry):
-        sa, sb = carry
-        normed = (conv[a] - mean2) * rstd2
-        level = normed * gain2 + shift2 + whole(xh, a).astype(f32)
-        value, slope = gelu_both(level)
-        put(zz, a, value.astype(bf))
-        gp = whole(ct, a).astype(f32) * slope
-        conv[a] = gp
-        put(ct, a, normed.astype(bf))
-        gm = tiles(gp) * real(a)[None]
-        return sa + jnp.sum(gm, axis=0), sb + jnp.sum(gm * tiles(normed), axis=0)
+    scale2 = rstd2 * gain2
+
+    def out_body(late):
+        def body(a, carry):
+            sa, sb = carry
+            centred = flat(conv[a]) - mean2
+            level = centred * scale2 + (shift2 + whole(fx, a).astype(f32))
+            value, slope = gelu_both(level)
+            land(xh, a, value.astype(bf))
+            gp = whole(ct, a).astype(f32) * slope
+            conv[a] = tiles(gp)
+            put(iz, a, centred.astype(bf))
+            gm = keep(gp, late)
+            return sa + down_rows(gm), sb + down_rows(gm * centred)
+
+        return body
 
     carry = (zero16, zero16)
     outs = []
@@ -560,62 +568,67 @@
         with jax.named_scope("cotangent_wait"):
             take_rows(ct, sem_c, j)
         with jax.named_scope("level_two"):
-            carry = lax.fori_loop(a0, a1, out_body, carry)
-        ship(zz, act_own, act_rcv, sem_a, j)
-
-    halo_out(1, [lambda a: conv[a], lambda a: whole(ct, a)])
+            carry = lax.fori_loop(a0, a1, out_body(a0 >= cut), carry)
+        ship(xh, act_own, act_rcv, sem_a, j)
+
     pad6 = jnp.zeros((6, C), f32)
     all_start(2, jnp.concatenate([row_sum(carry[0]), row_sum(carry[1]), pad6], axis=0))
+    halo_out(1, [lambda a: flat(conv[a]), lambda a: whole(iz, a)])
     with jax.named_scope("sum2"):
-        all_next(2, add_up)
+        all_more(2, add_up)
         halo_relay(1, 2)
-        all_more(2, add_up)
         sum2 = all_end(2, add_up)
-    out_scale = gain2 * rstd2
-    out_shift = out_scale * sum2[0:1] / count
-    out_slope = out_scale * sum2[1:2] / count
-
-    def back(grad, x, scale, shift, slope):
-        corr = tiles(x * slope + shift) * pw[None]
-        return grad * scale - corr.reshape(grad.shape)
-
-    def gconv_body(a, _):
-        gp = conv[a]
-        t = back(gp, whole(ct, a).astype(f32), out_scale, out_shift, out_slope)
-        gch[a + HALO] = tiles(times(t, real(a)).astype(bf))
-        put(ct, a, gp.astype(bf))
-        return 0
+    sum2 = scaled(sum2, rstd2)
+
+    def corrections(scale, rstd, sums):
+        shift = scale * sums[0:1] / count
+        slope = scale * rstd * sums[1:2] / count
+        return scale, (shift * pw)[None], (slope * pw)[None]
+
+    def back(grad, centred, scale, shift, slope):
+        return grad * scale - (tiles(centred) * slope + shift).reshape(grad.shape)
+
+    out_corr = corrections(scale2, rstd2, sum2)
+
+    def gconv_body(late):
+        def body(a, _):
+            gp = flat(conv[a])
+            t = back(gp, whole(iz, a).astype(f32), *out_corr)
+            gch[a + HALO] = tiles(keep(t, late).astype(bf))
+            put(iz, a, gp.astype(bf))
+            return 0
+
+        return body
 
     with jax.named_scope("gconv"):
-        lax.fori_loop(0, L, gconv_body, 0)
+        each(gconv_body, 0)
     halo_in(1, 2)
     fill_halo(
         gch,
-        lambda h: back(halo_r[1, h].astype(f32), halo_r[2, h].astype(f32), out_scale, out_shift, out_slope).astype(bf),
+        lambda h: back(halo_r[1, h].astype(f32), halo_r[2, h].astype(f32), *out_corr).astype(bf),
     )
 
-    def gact_block(a0, n, carry):
+    def gact_block(a0, late, carry):
         sa, sb = carry
+        n = len(late)
         t = jnp.zeros((n * R, C), f32)
         for tap in range(TAPS):
             t = t + lax.dot_general(
                 gch[pl.ds(a0 + TAPS - 1 - tap, n)].reshape(n * R, C), wt[tap], last, preferred_element_type=f32
             )
         for i in range(n):
-            centred = summed[a0 + i].reshape(R, C) - mean1
+            centred = flat(summed[a0 + i]) - mean1
             _, slope = gelu_both(centred * scale1 + shift1)
             gl = t[i * R : (i + 1) * R] * slope
-            conv[a0 + i] = gl
-            gm = tiles(gl) * real(a0 + i)[None]
-            sa = sa + jnp.sum(gm, axis=0)
-            sb = sb + jnp.sum(gm * tiles(centred * rstd1), axis=0)
+            conv[a0 + i] = tiles(gl)
+            gm = keep(gl, late[i])
+            sa = sa + down_rows(gm)
+            sb = sb + down_rows(gm * centred)
         return sa, sb
 
     with jax.named_scope("grad_act"):
         carry = blocks(gact_block, (zero16, zero16))
     all_start(3, jnp.concatenate([row_sum(carry[0]), row_sum(carry[1]), pad6], axis=0))
-    with jax.named_scope("sum1"):
-        all_next(3, add_up)
 
     def tap_body(tap, _):
         t = lax.dot_general(
@@ -629,14 +642,13 @@
         return 0
 
     with jax.named_scope("tap_grad"):
-        lax.fori_loop(0, TAPS // 2, tap_body, 0)
+        lax.fori_loop(0, EARLY // 2, tap_body, 0)
         all_more(3, add_up)
-        lax.fori_loop(TAPS // 2, TAPS, tap_body, 0)
+        lax.fori_loop(EARLY // 2, EARLY, tap_body, 0)
     with jax.named_scope("sum1_wait"):
         sum1 = all_end(3, add_up)
-    in_scale = gain1 * rstd1
-    in_shift = in_scale * sum1[0:1] / count
-    in_slope = in_scale * rstd1 * sum1[1:2] / count
+    sum1 = scaled(sum1, rstd1)
+    in_corr = corrections(scale1, rstd1, sum1)
 
     neighbour = (2 * chip + 1 - core, s)
     core_rows = pl.multiple_of(core * H, H)
@@ -645,18 +657,21 @@
         return pl.multiple_of(owned(t) * slice_rows, slice_rows)
 
     chip_rows = slice_of(c1)
-    spans = (pl.ds(0, TAPS), pl.ds(TAPS, 3))
+    spans = (pl.ds(0, EARLY), pl.ds(EARLY, TAPS + 3 - EARLY))
+
+    core_sends = []
 
     def grad_core(i):
         cut = (slice(None), spans[i])
-        go(
-            remote(
-                gb.at[(*cut, pl.ds(other_rows, H))], gb_core.at[cut], sem_g.at[0, i, 0], sem_g.at[1, i, 0], neighbour
-            )
+        cp = remote(
+            gb.at[(*cut, pl.ds(other_rows, H))], gb_core.at[cut], sem_g.at[0, i, 0], sem_g.at[1, i, 0], neighbour
         )
+        cp.start()
+        core_sends.append(cp)
 
     def grad_chips(i):
         cut = (slice(None), spans[i])
+        core_sends[i].wait_send()
         arrive(gb_core.at[cut], sem_g.at[1, i, 0])
         total = gb[(*cut, pl.ds(core_rows, H))] + gb_core[cut]
         gb_low[cut] = total.astype(bf)
@@ -679,7 +694,7 @@
             arrive(gb_chips.at[(lax.rem(c1 + z.p1 - d, z.p1), *cut)], sem_g.at[1, i, d])
         gb_sum[cut] = add_up([gb_chips[(p, *cut)].astype(f32) for p in range(z.p1)])
         if z.p2 > 1:
-            gb_far[(c2, *cut)] = gb_sum[cut]
+            gb_far[(c2, *cut)] = gb_sum[cut].astype(bf)
             for d in range(1, z.p2):
                 t = lax.rem(c2 + d, z.p2)
                 go(
@@ -693,7 +708,7 @@
                 )
             for d in range(1, z.p2):
                 arrive(gb_far.at[(lax.rem(c2 + z.p2 - d, z.p2), *cut)], sem_g.at[1, i, 24 + d])
-            gb_sum[cut] = add_up([gb_far[(p, *cut)] for p in range(z.p2)])
+            gb_sum[cut] = add_up([gb_far[(p, *cut)].astype(f32) for p in range(z.p2)])
         go(remote(gb_sum.at[o, spans[i]], gb_pair.at[spans[i]], sem_g.at[0, i, 8], sem_g.at[1, i, 8], across))
 
     def grad_back(i):
@@ -701,8 +716,8 @@
         mine = gb_sum[s, spans[i]]
         other = gb_pair[spans[i]]
         own = pl.multiple_of(core_rows + chip_rows, slice_rows)
-        gb_all[spans[i], pl.ds(own, slice_rows)] = mine + other
-        at = gb_all.at[spans[i], pl.ds(own, slice_rows)]
+        gb[0, spans[i], pl.ds(own, slice_rows)] = mine + other
+        at = gb.at[0, spans[i], pl.ds(own, slice_rows)]
         for d in range(1, z.p1):
             t = lax.rem(c1 + d, z.p1)
             go(remote(at, at, sem_g.at[0, i, 8 + d], sem_g.at[1, i, 8 + d], peer_b(t)))
@@ -711,81 +726,113 @@
         for d in range(1, z.p1):
             t = lax.rem(c1 + z.p1 - d, z.p1)
             at = pl.multiple_of(core_rows + slice_of(t), slice_rows)
-            arrive(gb_all.at[spans[i], pl.ds(at, slice_rows)], sem_g.at[1, i, 8 + d])
-        at = gb_all.at[spans[i], pl.ds(core_rows, H)]
+            arrive(gb.at[0, spans[i], pl.ds(at, slice_rows)], sem_g.at[1, i, 8 + d])
+        at = gb.at[0, spans[i], pl.ds(core_rows, H)]
         go(remote(at, at, sem_g.at[0, i, 16], sem_g.at[1, i, 16], neighbour))
 
     def grad_done(i):
-        arrive(gb_all.at[spans[i], pl.ds(other_rows, H)], sem_g.at[1, i, 16])
+        arrive(gb.at[0, spans[i], pl.ds(other_rows, H)], sem_g.at[1, i, 16])
 
     grad_core(0)
 
-    def input_body(a, _):
-        gs = back(conv[a], summed[a].reshape(R, C) - mean1, in_scale, in_shift, in_slope)
-        gs = times(gs, real(a)).astype(bf)
-        gch[a + HALO] = tiles(gs)
-        parts[0] = gs.astype(f32).reshape(J, RW, C)
-        link(lambda v: parts[0, v], 1)
+    def grad_body(late):
+        def body(a, _):
+            gs = back(flat(conv[a]), flat(summed[a]) - mean1, *in_corr)
+            gs = keep(gs, late).astype(bf)
+            conv[a] = tiles(gs.astype(f32))
+            return 0
+
+        return body
+
+    with jax.named_scope("grad_sum"):
+        each(grad_body, 0)
+
+    def input_chunk(j):
+        a0, a1 = z.chunks[j]
+        n = a1 - a0
+        span = pl.ds(a0, n)
+        summed[span, 0] = jnp.zeros((n, RW, C), f32)
+        for v in range(J - 1, 0, -1):
+            summed[span, v] = conv[span, v] * edge[1, v : v + 1] + summed[span, kin[0, v]]
         for w in range(J):
-            at = slice(w * RW, (w + 1) * RW)
-            mixed[0, at] = (parts[0, w] * edge[0, w : w + 1]).astype(bf)
-            mixed[1, at] = chain[kin[1, w]].astype(bf)
-            mixed[2, at] = (parts[0, par[w]] * edge[2, w : w + 1]).astype(bf)
-        t = whole(ct, a).astype(f32)
-        for k in range(3):
-            t = t + lax.dot_general(mixed[k], ws[:, k * C : (k + 1) * C], last, preferred_element_type=f32)
-        put(iz, a, t.astype(bf))
-        return 0
-
-    for j, (a0, a1) in enumerate(z.chunks):
-        with jax.named_scope("input_grad"):
-            lax.fori_loop(a0, a1, input_body, 0)
+            mixed[0, pl.ds(0, n), w] = summed[span, kin[1, w]].astype(bf)
+            mixed[1, pl.ds(0, n), w] = (conv[span, par[w]] * edge[2, w : w + 1]).astype(bf)
+
+        def out(i, _):
+            t = whole(iz, a0 + i).astype(f32)
+            own = (conv[a0 + i] * edge[0][:, None, :]).astype(bf)
+            for k, rows in enumerate((own, mixed[0, i], mixed[1, i])):
+                t = t + lax.dot_general(
+                    flat(rows), ws[:, k * C : (k + 1) * C], last, preferred_element_type=f32
+                )
+            put(iz, a0 + i, t.astype(bf))
+            return 0
+
+        lax.fori_loop(0, n, out, 0)
+
         ship(iz, ing_own, ing_rcv, sem_i, j)
-        with jax.named_scope("grad_reduce"):
-            if j == 0:
-                grad_chips(0)
-            if j == n_chunks - 1:
-                grad_pair(0)
 
     def edge_rows_f(v):
         return jnp.concatenate(
-            [xh[0, :, pl.ds(v, 1)].reshape(L * RW, H), xh[1, :, pl.ds(v, 1)].reshape(L * RW, H)], axis=1
+            [fx[0, :, pl.ds(v, 1)].reshape(L * RW, H), fx[1, :, pl.ds(v, 1)].reshape(L * RW, H)], axis=1
         )
 
     def edge_rows_g(v):
-        return gch[pl.ds(HALO, L), pl.ds(v, 1)].reshape(L * RW, C)
-
-    sg[...] = jnp.zeros_like(sg)
-
-    def edge_body(v, acc):
-        pv = par[v]
-        hot = jnp.where(lax.broadcasted_iota(jnp.int32, (8, C), 1) == v, 1.0, 0.0)
-        kind = lax.broadcasted_iota(jnp.int32, (8, C), 0)
-        far = jnp.where(v > 0, 1.0, 0.0)
-        f_v, g_v = edge_rows_f(v), edge_rows_g(v)
-        f_p, g_p = edge_rows_f(pv), edge_rows_g(pv)
-        for k, (fx, gx, on) in enumerate(((f_v, g_v, 1.0), (f_p, g_v, far), (f_v, g_p, far))):
-            prod = lax.dot_general(fx, gx, first, preferred_element_type=f32)
-            sg[k] = sg[k] + prod * edge[k, pl.ds(v, 1)]
-            dot = jnp.sum(row_sum(prod * ws[:, k * C : (k + 1) * C].astype(f32)), axis=1, keepdims=True)
-            acc = acc + jnp.where(kind == k, hot, 0.0) * (dot * on)
-        return acc
-
+        return conv[:, pl.ds(v, 1)].reshape(L * RW, C).astype(bf)
+
+    gb[:, TAPS:] = jnp.zeros((2, 3, C, H), f32)
+
+    dots[...] = jnp.zeros_like(dots)
+    unroll = 5 if J % 5 == 0 else 1
+
+    def edge_body(i, _):
+        for u in range(unroll):
+            v = i * unroll + u
+            pv = par[v]
+            f_v, f_p, g_v, g_p = edge_rows_f(v), edge_rows_f(pv), edge_rows_g(v), edge_rows_g(pv)
+            both = lax.dot_general(
+                f_v, jnp.concatenate([g_v, g_p], axis=1), first, preferred_element_type=f32
+            )
+            up_prod = lax.dot_general(f_p, g_v, first, preferred_element_type=f32)
+            for k, prod in enumerate((both[:, :C], up_prod, both[:, C:])):
+                part = prod * edge[k, pl.ds(v, 1)]
+                for h in range(2):
+                    j = 2 * k + h
+                    gb[j // 3, TAPS + j % 3] += part[:, h * H : (h + 1) * H]
+                dots[k, pl.ds(v, 1)] = row_sum(prod * ws[:, k * C : (k + 1) * C].astype(f32))
+        return 0
+
+    def edges():
+        lax.fori_loop(0, J // unroll, edge_body, 0)
+        ones = jnp.ones((8, C), f32)
+        rows = [
+            lax.dot_general(ones, dots[k], last, precision=exact_mode, preferred_element_type=f32)[0:1]
+            for k in range(3)
+        ]
+        val = jnp.concatenate(rows + [jnp.zeros((5, H), f32)], axis=0)
+        return jnp.concatenate([val, jnp.zeros((8, C - H), f32)], axis=1)
+
+    input_chunk(0)
+    grad_chips(0)
+    with jax.named_scope("tap_grad_late"):
+        lax.fori_loop(EARLY, TAPS, tap_body, 0)
+    for j in range(1, n_chunks // 2):
+        input_chunk(j)
+    grad_pair(0)
     with jax.named_scope("edges"):
-        dvec = lax.fori_loop(0, J, edge_body, jnp.zeros((8, C), f32))
-    for j in range(6):
-        k, h = j // 2, j % 2
-        gb[j // 3, TAPS + j % 3] = sg[k, :, h * H : (h + 1) * H]
+        dvec = edges()
     grad_core(1)
-    all_start(4, dvec)
+    for j in range(n_chunks // 2, n_chunks):
+        input_chunk(j)
+        if j == n_chunks // 2:
+            grad_chips(1)
+            all_start(4, dvec)
+            grad_back(0)
     with jax.named_scope("grad_reduce"):
-        grad_back(0)
-        grad_chips(1)
-        all_next(4, add_up)
+        grad_pair(1)
         all_more(4, add_up)
-        grad_pair(1)
+        grad_last(0)
         grad_back(1)
-        grad_last(0)
         dvec = all_end(4, add_up)
         grad_last(1)
     for k in range(3):
@@ -801,10 +848,10 @@
     with jax.named_scope("grad_reduce_end"):
         grad_done(0)
         grad_done(1)
-        last_out = [pltpu.make_async_copy(gb_all.at[pl.ds(0, TAPS)], tg_out, sem_l.at[2, 2])]
+        last_out = [pltpu.make_async_copy(gb.at[0, pl.ds(0, TAPS)], tg_out, sem_l.at[2, 2])]
         for j in range(3):
             last_out.append(
-                pltpu.make_async_copy(gb_all.at[TAPS + j], sg_out.at[:, pl.ds(j * H, H)], sem_l.at[2, 3 + j])
+                pltpu.make_async_copy(gb.at[0, TAPS + j], sg_out.at[:, pl.ds(j * H, H)], sem_l.at[2, 3 + j])
             )
         for cp in last_out:
             cp.start()
@@ -840,7 +887,8 @@
     r2,
     r3,
     ig_out,
-    low,
+    low_act,
+    low_ing,
     full,
     tg,
     sg,
@@ -849,10 +897,10 @@
 ):
     J, L = z.joints, z.blk
     s = lax.axis_index("sub")
-    jobs = [(act_own, act_out, s), (ing_own, ing_out, s), (act_rcv, act_out, 1 - s), (ing_rcv, ing_out, 1 - s)]
+    jobs = [(act_own, act_out, s), (act_rcv, act_out, 1 - s), (ing_own, ing_out, s), (ing_rcv, ing_out, 1 - s)]
     ins = []
     for i, (src, _, _) in enumerate(jobs):
-        cp = pltpu.make_async_copy(src, low.at[i], sem_in.at[i])
+        cp = pltpu.make_async_copy(src, (low_act if i < 2 else low_ing).at[i % 2], sem_in.at[i])
         cp.start()
         ins.append(cp)
     grads = []
@@ -864,6 +912,8 @@
         r[...] = sums_in[i : i + 1]
     ig_out[...] = ig_in[...]
     cut = L - z.pad
+    fr = full.reshape(4, L, J, RW, z.half)
+    lows = (low_act.reshape(2, L, J, RW, z.half), low_ing)
 
     def pieces(i, dst, w):
         for part, (a0, a1) in enumerate(z.locals):
@@ -879,8 +929,7 @@
         ins[i].wait()
 
         def body(a, _, i=i):
-            value = low[i, a].reshape(z.rows, z.half).astype(jnp.float32)
-            full[i, a] = value.reshape(J, NB, 2, z.half)
+            fr[i, a] = lows[i // 2][i % 2, a].astype(jnp.float32)
             return 0
 
         lax.fori_loop(0, L, body, 0)
@@ -914,40 +963,39 @@
         return x.transpose(0, 2, 3, 1, 4).reshape(frames, joints, 2, half)
 
     any_, vmem, smem = (pl.BlockSpec(memory_space=m) for m in (pl.ANY, pltpu.VMEM, pltpu.SMEM))
-    blocked = (L, J, NB, 2, H)
+    landing = (L, J, NB, 2, H)
+    blocked = (L, J, RW, H)
     sds = jax.ShapeDtypeStruct
     VM, DMA = pltpu.VMEM, pltpu.SemaphoreType.DMA
     nch = len(z.chunks)
     outs = pl.pallas_call(
         functools.partial(mega, z),
         name="graph_conv_block",
-        out_shape=[sds(blocked, bf)] * 4
+        out_shape=[sds(landing, bf)] * 2
+        + [sds(blocked, bf)] * 2
         + [sds((TAPS, C, H), f32), sds((C, 3 * H), f32), sds((8, H), f32), sds((3, J, J), f32)],
         in_specs=[any_] * 4 + [vmem, smem, smem] + [vmem] * 4,
         out_specs=[any_] * 6 + [vmem] * 2,
         scratch_shapes=[
-            VM((2,) + blocked, bf),
+            VM((2,) + landing, bf),
+            VM((2,) + landing, bf),
             VM((2,) + blocked, bf),
             VM((TAPS, C, C), bf),
             VM((C, 3 * C), bf),
-            VM((3, J, RW, C), f32),
-            VM((J, RW, C), f32),
-            VM((3, R, C), bf),
             VM((L, J, RW, C), f32),
             VM((L + 2 * HALO, J, RW, C), bf),
-            VM((L, R, C), f32),
+            VM((L, J, RW, C), f32),
             VM((L + 2 * HALO, J, RW, C), bf),
-            VM((2,) + blocked, bf),
             VM((2,) + blocked, bf),
             VM((2, TAPS + 3, C, H), f32),
             VM((2, TAPS + 3, H, H), f32),
             VM((2, TAPS + 3, H, H), bf),
             VM((z.p1, 2, TAPS + 3, H // z.p1, H), bf),
-            VM((z.p2, 2, TAPS + 3, H // z.p1, H), f32),
+            VM((z.p2, 2, TAPS + 3, H // z.p1, H), bf),
             VM((2, TAPS + 3, H // z.p1, H), f32),
             VM((TAPS + 3, H // z.p1, H), f32),
-            VM((TAPS + 3, C, H), f32),
-            VM((3, C, C), f32),
+            VM((2, max(a1 - a0 for a0, a1 in z.chunks), J, RW, C), bf),
+            VM((3, H, C), f32),
             VM((2, 8, H), f32),
             VM((3, J, J), f32),
             VM((3, J, C), f32),
@@ -955,9 +1003,8 @@
             VM((3, HALO, 64, C), bf),
             VM((3, HALO, 64, C), bf),
             VM((3, HALO, 64, C), bf),
-            VM((5, 4, 8, C), f32),
-            VM((5, z.q1, 8, C), f32),
-            VM((5, z.q2, 8, C), f32),
+            VM((5, z.near, 8, C), f32),
+            VM((5, z.p2, 8, C), f32),
             VM((5, 2, 8, C), f32),
             DMA((3, 2 * NB)),
             DMA((2, nch, NB)),
@@ -967,13 +1014,12 @@
             DMA((2, 40)),
             DMA((2, 2, 2)),
             DMA((2, 2, 32)),
-            DMA((2, 5, 4)),
-            DMA((2, 5, z.q1)),
-            DMA((2, 5, z.q2)),
+            DMA((2, 5, z.near)),
+            DMA((2, 5, z.p2)),
             DMA((2, 5)),
         ],
         compiler_params=pltpu.CompilerParams(
-            collective_id=0, has_side_effects=True, vmem_limit_bytes=62 * 2**20
+            collective_id=0, has_side_effects=True, vmem_limit_bytes=63 * 2**20
         ),
     )(
         natural(features),
@@ -995,8 +1041,9 @@
         in_specs=[any_] * 6 + [vmem] * 2,
         out_specs=[any_] * 4 + [vmem] * 5,
         scratch_shapes=[
-            VM((4,) + blocked, bf),
-            VM((4,) + blocked, f32),
+            VM((2,) + landing, bf),
+            VM((2,) + blocked, bf),
+            VM((4,) + landing, f32),
             VM((TAPS, C, H), f32),
             VM((C, 3 * H), f32),
             DMA((8,)),

time: 234 us -> 215 us (0.919)
  Pallas kernels: 233 us -> 214 us
    pallas_call x1, Pallas kernels: 221 us -> 204 us  [block(): pl.pallas_call(functools.partial(mega, z), name='graph_conv_block', out_s...]
where the time goes in v3:
time: 215 us
  Pallas kernels  214 us (100%)
    pallas_call x1, Pallas kernels, block(): pl.pallas_call(functools.partial(mega, z), name='graph_conv_block', out_s...  204 us
    pallas_call x1, Pallas kernels, block(): pl.pallas_call(functools.partial(finish, z), name='natural_order', out_sh...  10.8 us

profile of v3, /device:TPU:1, one launch (start us, length us, event | category | flops | bytes accessed | tf_op | source)
XLA Modules:
  0.0 215.2 jit_solution(15343594586173554333)
XLA Ops:
  0.6 203.6 %graph_conv_block.1 = (bf16[19,25,8,2,128]{4,3,2,1,0:T(2,128)(2,1)}, bf16[19,25,8,2,128]{4,3,2,1,0:T(2,128)(2,1)}, bf16[19,25,16,128]{3,2,1,0:T(8,128)(2,1)}, bf...) custom-call(bf16[300,25,2,128]{3,2,1,0:T(2,128)(2,1)} %bitcast.20, ...), custom_call_target="tpu_custom_call" | custom-call | tf_op jit(solution)/shard_map/graph_conv_block/pallas_call | solution.py:971
  204.3 10.8 %natural_order.1 = (f32[300,25,2,128]{3,2,1,0:T(2,128)}, f32[300,25,2,128]{3,2,1,0:T(2,128)}, f32[9,256,128]{2,1,0:T(8,128)}, f32[256,384]{1,0:T(8,128)}, f32[1,...) custom-call(bf16[19,25,8,2,128]{4,3,2,1,0:T(2,128)(2,1)} %get-tuple-element.26, ...), custom_call_target="tpu_custom_call" | custom-call | tf_op jit(solution)/shard_map/natural_order/pallas_call | solution.py:1034
